TPU v7x, 128 devices: a whole 4x4x4 slice. The times are simulated.
128 devices in a mesh: resp: 8 (over z, core), expert: 4 (over x), prompt: 4 (over y).
Axes of the slice: x: 4, y: 4, z: 4, core: 2. Of those that a mesh axis runs over, the one named last changes fastest.
Arguments:
- hidden: bfloat16 [256, 7168], P(('prompt', 'resp'), 'expert'), parts along dimension 0, may hold values from -6 to 6
- queries: bfloat16 [256, 128, 576], P(('prompt', 'resp'), 'expert'), parts along dimension 0, may hold values from -128 to 128
- new_latents: bfloat16 [256, 576], P(('prompt', 'resp')), parts along dimension 0, may hold values from -6 to 6
- suffix_cache: bfloat16 [64, 512, 576], P(('prompt', 'resp')), parts along dimension 0, may hold values from -6 to 6
- suffix_lengths: int32 [64], P(('prompt', 'resp')), parts along dimension 0, may hold values from 1 to 512, 6144 in all
- prompt_latents: bfloat16 [131072, 576], P(('prompt', 'resp', 'expert')), parts along dimension 0, may hold values from -6 to 6
- value_up: bfloat16 [128, 512, 128], P('expert'), may hold values from -0.25 to 0.25
- out_proj: bfloat16 [128, 128, 7168], P('expert', 'resp'), may hold values from -0.0625 to 0.0625
- rms_gain: float32 [7168], replicated, may hold values from 0.1 to 1.9
- gate_ids: int32 [256, 2], P('prompt'), parts along dimension 0, may hold values from 0 to 3, all different within a row
- gate_weights: float32 [256, 2], P('prompt'), parts along dimension 0, may hold values from 0.1 to 1
- w_gate: bfloat16 [4, 7168, 2048], P('expert', None, 'resp'), may hold values from -0.0625 to 0.0625
- w_up: bfloat16 [4, 7168, 2048], P('expert', None, 'resp'), may hold values from -0.0625 to 0.0625
- w_down: bfloat16 [4, 2048, 7168], P('expert', 'resp'), may hold values from -0.1875 to 0.1875
Outputs:
- attended: bfloat16 [256, 7168], P(('prompt', 'resp'), 'expert'), parts along dimension 0
- layer_out: bfloat16 [256, 7168], P(('prompt', 'resp'), 'expert'), parts along dimension 0
There are 4 independent parts, one for each index of `prompt`. A program takes and returns all parts, laid end to end along the dimension named above; an argument that names none is the same for every part. Nothing has to cross between parts.
Inputs may be any that keep to these rules, and one draw needn't show every extreme that they name: `suffix_lengths`: each response has 1 to 512 live cache slots; some response has exactly 512. `gate_ids`: each token names 2 different experts.
All inputs are finite; a program needn't handle non-finite values. No bound on the sum of `suffix_lengths` on one device may be relied on, other than what follows from the above.
Results may differ from a plain program's by a relative error of at most 0.03.
Values may be sent and summed in bfloat16 or wider, within the bound.
A program may use at most 256 MiB of HBM per device.

v0:
```python
import math

import jax
import jax.numpy as jnp
from jax import lax
from jax.sharding import PartitionSpec as P

LAT = 512
ROPE = 64
NOPE = 128


def score_factor():
    return (NOPE + ROPE) ** (-0.5)


def online_step(state, query_rows, block):
    run_max, run_sum, run_acc = state
    scores = (
        lax.dot_general(
            query_rows, block, (((1,), (1,)), ((), ())), preferred_element_type=jnp.float32
        )
        * score_factor()
    )
    new_max = jnp.maximum(run_max, jnp.max(scores, axis=1))
    shrink = jnp.exp(run_max - new_max)
    weights = jnp.exp(scores - new_max[:, None])
    run_sum = run_sum * shrink + jnp.sum(weights, axis=1)
    run_acc = run_acc * shrink[:, None] + jnp.dot(
        weights.astype(jnp.bfloat16), block[:, :LAT], preferred_element_type=jnp.float32
    )
    return (new_max, run_sum, run_acc)


def fold_rows(state, query_rows, piece):
    row_count = piece.shape[0]
    width = math.gcd(row_count, 1024)
    blocks = piece.reshape(row_count // width, width, piece.shape[1])

    def advance(carry, block):
        return (online_step(carry, query_rows, block), None)

    state, ignored = lax.scan(advance, state, blocks)
    return state


def local_part(queries, new_latents, suffix_cache, suffix_lengths):
    owners = suffix_cache.shape[0]
    heads_here = queries.shape[1]
    steps_count = new_latents.shape[0] // owners
    query_rows = queries.reshape(owners, steps_count * heads_here, queries.shape[2])
    fresh_keys = new_latents.reshape(owners, steps_count, new_latents.shape[1])
    cache_scores = (
        jnp.einsum("brc,bkc->brk", query_rows, suffix_cache, preferred_element_type=jnp.float32)
        * score_factor()
    )
    own_scores = (
        jnp.einsum("brc,bkc->brk", query_rows, fresh_keys, preferred_element_type=jnp.float32)
        * score_factor()
    )
    cache_live = (
        jnp.arange(suffix_cache.shape[1], dtype=jnp.int32)[None, None, :]
        < suffix_lengths[:, None, None]
    )
    row_step = jnp.arange(steps_count * heads_here, dtype=jnp.int32) // heads_here
    own_live = (jnp.arange(steps_count, dtype=jnp.int32)[None, :] <= row_step[:, None])[None]
    cache_scores = jnp.where(cache_live, cache_scores, -jnp.inf)
    own_scores = jnp.where(own_live, own_scores, -jnp.inf)
    local_max = jnp.maximum(jnp.max(cache_scores, axis=2), jnp.max(own_scores, axis=2))
    cache_weights = jnp.exp(cache_scores - local_max[:, :, None])
    own_weights = jnp.exp(own_scores - local_max[:, :, None])
    local_sum = jnp.sum(cache_weights, axis=2) + jnp.sum(own_weights, axis=2)
    local_acc = jnp.einsum(
        "brk,bkc->brc",
        cache_weights.astype(jnp.bfloat16),
        suffix_cache[:, :, :LAT],
        preferred_element_type=jnp.float32,
    )
    local_acc = local_acc + jnp.einsum(
        "brk,bkc->brc",
        own_weights.astype(jnp.bfloat16),
        fresh_keys[:, :, :LAT],
        preferred_element_type=jnp.float32,
    )
    return (local_max.reshape(-1), local_sum.reshape(-1), local_acc.reshape(-1, LAT))


def on_device(
    hidden,
    queries,
    new_latents,
    suffix_cache,
    suffix_lengths,
    prompt_latents,
    value_up,
    out_proj,
    rms_gain,
    gate_ids,
    gate_weights,
    w_gate,
    w_up,
    w_down,
):
    tok_here, heads_here, latent_width = queries.shape
    local_state = local_part(queries, new_latents, suffix_cache, suffix_lengths)
    query_rows = queries.reshape(tok_here * heads_here, latent_width)
    run_max, run_sum, run_acc = fold_rows(
        local_state,
        query_rows,
        lax.all_gather(prompt_latents, ("resp", "expert"), axis=0, tiled=True),
    )
    run_sum = run_sum.reshape(tok_here, heads_here)
    run_acc = run_acc.reshape(tok_here, heads_here, LAT)
    context = (run_acc / run_sum[:, :, None]).astype(jnp.bfloat16)
    head_out = jnp.einsum(
        "thc,hcv->thv", context, value_up, preferred_element_type=jnp.float32
    ).astype(jnp.bfloat16)
    swapped = lax.all_to_all(head_out, "resp", split_axis=2, concat_axis=0, tiled=True)
    n_resp = lax.axis_size("resp")
    n_expert = lax.axis_size("expert")
    all_rows = swapped.shape[0]
    group_rows = all_rows // n_resp
    token_grid = swapped.reshape(n_resp, group_rows, swapped.shape[1] * swapped.shape[2])
    proj_grid = out_proj.reshape(
        out_proj.shape[0] * out_proj.shape[1], n_expert, out_proj.shape[2] // n_expert
    )
    out_terms = jnp.einsum(
        "gtk,kef->getf", token_grid, proj_grid, preferred_element_type=jnp.float32
    )
    out_terms = out_terms.reshape(n_resp * n_expert, group_rows, out_terms.shape[3])
    attended = (
        lax.psum_scatter(
            out_terms.astype(jnp.bfloat16), ("resp", "expert"), scatter_dimension=0, tiled=True
        )
        .astype(jnp.float32)[0]
        .astype(jnp.bfloat16)
    )
    resid = (hidden.astype(jnp.float32) + attended.astype(jnp.float32)).astype(jnp.bfloat16)
    everyone = lax.all_gather(resid[None], ("resp", "expert"), axis=0, tiled=True)
    stream_grid = everyone.reshape(n_resp, n_expert, group_rows, everyone.shape[2]).astype(
        jnp.float32
    )
    mean_square = jnp.mean(stream_grid * stream_grid, axis=(1, 3))
    gain_grid = rms_gain.reshape(n_expert, -1)
    normed = (
        stream_grid * lax.rsqrt(mean_square + 1e-06)[:, None, :, None] * gain_grid[None, :, None, :]
    ).astype(jnp.bfloat16)
    hidden_here = w_gate.shape[2]
    gate_grid = w_gate[0].reshape(n_expert, -1, hidden_here)
    up_grid = w_up[0].reshape(n_expert, -1, hidden_here)
    gate_value = jnp.einsum("getf,efh->gth", normed, gate_grid, preferred_element_type=jnp.float32)
    up_value = jnp.einsum("getf,efh->gth", normed, up_grid, preferred_element_type=jnp.float32)
    activation = (jax.nn.silu(gate_value) * up_value).astype(jnp.bfloat16)
    expert_here = lax.axis_index("expert")
    picked = (gate_ids == expert_here).astype(jnp.float32)
    share = 2.5 * jnp.sum(gate_weights * picked, axis=1) / jnp.sum(gate_weights, axis=1)
    share = share.reshape(n_resp, group_rows)
    down_grid = w_down[0].reshape(hidden_here, n_expert, -1)
    moe_terms = (
        jnp.einsum("gth,hef->getf", activation, down_grid, preferred_element_type=jnp.float32)
        * share[:, None, :, None]
    )
    moe_terms = moe_terms.reshape(n_resp * n_expert, group_rows, moe_terms.shape[3])
    moe = lax.psum_scatter(
        moe_terms.astype(jnp.bfloat16), ("resp", "expert"), scatter_dimension=0, tiled=True
    ).astype(jnp.float32)[0]
    layer_out = (resid.astype(jnp.float32) + moe).astype(jnp.bfloat16)
    return (attended, layer_out)


def solution(mesh):
    placed = (
        P(("prompt", "resp"), "expert"),
        P(("prompt", "resp"), "expert", None),
        P(("prompt", "resp"), None),
        P(("prompt", "resp"), None, None),
        P(("prompt", "resp")),
        P(("prompt", "resp", "expert"), None),
        P("expert", None, None),
        P("expert", "resp", None),
        P(),
        P("prompt", None),
        P("prompt", None),
        P("expert", None, "resp"),
        P("expert", None, "resp"),
        P("expert", "resp", None),
    )
    return jax.shard_map(
        on_device,
        mesh=mesh,
        in_specs=placed,
        out_specs=(P(("prompt", "resp"), "expert"), P(("prompt", "resp"), "expert")),
        check_vma=False,
    )
```

profile of v0, /device:TPU:1, one launch (start us, length us, event | category | flops | bytes accessed | tf_op | source)
XLA Modules:
  0.0 523.4 jit_solution(11367971083349360701)
XLA Ops:
  10.6 1.8 fusion.54
  13.5 125.3 %all-gather.3.cloned.1.call-done = bf16[32768,576]{0,1:T(8,128)(2,1)} async-done(((bf16[1024,576]{0,1:T(8,128)(2,1)}), bf16[32768,576]{0,1:T(8,128)(2,1)}) %all-gather.3.cloned.1.call-update) | async-done | bytes 37748752 | tf_op jit(solution)/shard_map/all_gather | solution.py:110
  138.8 51.6 %copy.70 = bf16[32768,576]{1,0:T(8,128)(2,1)} copy(bf16[32768,576]{0,1:T(8,128)(2,1)} %all-gather.3.cloned.1.call-done) | data formatting | bytes 75497472 | tf_op jit(solution)/shard_map/all_gather | solution.py:110
  190.4 93.8 %while.14 = (s32[]{:T(128)}, f32[256]{0:T(256)S(1)}, f32[256]{0:T(256)S(1)}, f32[256,512]{1,0:T(8,128)S(1)}, bf16[32,1024,576]{2,1,0:T(8,128)(2,1)}, /*index=5*/bf16[256,576]{1,0:T(8,128)(2,1)S(1)}, s32[]{:T(128)}) while((s32[]{:T(128)}, f32[256]{0:T(256)S(1)}, f32[256]{0:T(256)S(1)}, f32[256,512]{1,0:T(8,128)S(1)}, ...), condition=%wide.region_7.8_spmd, body=%wide.region_4.7_spmd.sunk | while | flops 572260864 | bytes 9093201 | solution.py:43
  193.4 1.4 dynamic-slice_bitcast_fusion.2
  196.3 1.4 dynamic-slice_bitcast_fusion.2
  199.2 1.4 dynamic-slice_bitcast_fusion.2
  202.2 1.4 dynamic-slice_bitcast_fusion.2
  205.1 1.4 dynamic-slice_bitcast_fusion.2
  208.0 1.4 dynamic-slice_bitcast_fusion.2
  211.0 1.4 dynamic-slice_bitcast_fusion.2
  213.9 1.4 dynamic-slice_bitcast_fusion.2
  216.8 1.4 dynamic-slice_bitcast_fusion.2
  219.7 1.4 dynamic-slice_bitcast_fusion.2
  284.4 3.0 fusion.25
  288.5 3.6 all-to-all-start
  292.2 14.1 %reshape.137 = bf16[512,4,1792]{2,1,0:T(4,128)(2,1)} reshape(bf16[32,16,7168]{2,1,0:T(8,128)(2,1)} %param.23) | data formatting | bytes 14680064 | tf_op jit(solution)/shard_map/reshape | solution.py:124
  307.5 5.4 %fusion.17 = bf16[8,8,4,1792]{3,1,2,0:T(8,128)(2,1)} fusion(bf16[512,4,1792]{2,1,0:T(4,128)(2,1)} %reshape.137, bf16[8,8,512,1]{2,1,0,3:T(8,128)(2,1)S(1)} %reshape.141), kind=kOutput, calls=%fused_computation.18 | convolution fusion | flops 470220800 | bytes 8323072 | tf_op jit(solution)/shard_map/gtk,kef->getf/dot_general | solution.py:127
  313.3 7.7 %reshape_squeeze.11 = bf16[256,4,1792]{2,1,0:T(4,128)(2,1)} reshape(bf16[1,256,7168]{2,1,0:T(8,128)(2,1)} %param.29) | data formatting | bytes 7340032 | tf_op jit(solution)/shard_map/reshape;squeeze | solution.py:158
  321.0 66.1 %reduce-scatter.3.cloned.1.call-done = bf16[1,8,1792]{2,1,0:T(8,128)(2,1)} async-done(((bf16[32,8,1792]{2,1,0:T(8,128)(2,1)}), bf16[1,8,1792]{2,1,0:T(8,128)(2,1)}) %reduce-scatter.3.cloned.1.call-update) | async-done | bytes 28688 | tf_op jit(solution)/shard_map/reduce_scatter | solution.py:132
  387.9 44.1 %all-gather = bf16[256,1792]{1,0:T(8,128)(2,1)S(1)} all-gather(bf16[8,1792]{1,0:T(8,128)(2,1)S(1)} %add_convert_fusion), channel_id=2, replica_groups=mesh['resp'=8,'expert'=4,'prompt'=4] {'resp','expert'}, dimensions={0}, use_global_device_ids=true | all-gather | bytes 946176 | tf_op jit(solution)/shard_map/all_gather | solution.py:139
  432.6 2.8 convolution_bitcast_fusion.1
  435.4 6.3 %fusion.14 = bf16[8,8,4,1792]{3,1,2,0:T(8,128)(2,1)} fusion(bf16[256,4,1792]{2,1,0:T(4,128)(2,1)} %reshape_squeeze.11, f32[8,8]{1,0:T(8,128)S(1)} %div.47, bf16[8,4,8,1792]{3,2,1,0:T(8,128)(2,1)S(1)} %bitcast.103, bf16[4,1792,256,1]{2,1,0,3:T(8,128)(2,1)} %bitcast.95, f32[8,8,256]{2,1,0:T(8,128)S(1)} %convolution_bitcast_fusion.1), kind=kOutput, calls=%fused_computation.17 | convolution fusion | flops 470777856 | bytes 9240832 | tf_op jit(solution)/shard_map/gth,hef->getf/dot_general | solution.py:160
  441.7 73.8 %reduce-scatter.5.cloned.1.call-done = bf16[1,8,1792]{2,1,0:T(8,128)(2,1)} async-done(((bf16[32,8,1792]{2,1,0:T(8,128)(2,1)}), bf16[1,8,1792]{2,1,0:T(8,128)(2,1)}) %reduce-scatter.5.cloned.1.call-update) | async-done | bytes 28688 | tf_op jit(solution)/shard_map/reduce_scatter | solution.py:164
  (264 shorter events, 88.0 us)
Async XLA Ops:
  7.2 5.8 %copy-start.1 = (bf16[2,512,576]{1,2,0:T(8,128)(2,1)S(1)}, bf16[2,512,576]{1,2,0:T(8,128)(2,1)}, u32[]{:S(2)}) copy-start(bf16[2,512,576]{1,2,0:T(8,128)(2,1)} %param.19) | copy-start | bytes 3538948
  7.2 131.6 %all-gather.3.cloned.1.call-start = ((), (), s32[]{:S(2)}) async-start(), calls=%async_computation.3 | async-start | bytes 38928384 | tf_op jit(solution)/shard_map/all_gather | solution.py:110
  13.5 177.0 %copy-start = (bf16[8,32,576]{2,1,0:T(8,128)(2,1)S(1)}, bf16[8,32,576]{2,1,0:T(8,128)(2,1)}, u32[]{:S(2)}) copy-start(bf16[8,32,576]{2,1,0:T(8,128)(2,1)} %param.17) | copy-start | bytes 884740
  288.5 17.7 %all-to-all-start = ((bf16[8,2,2048]{2,1,0:T(2,128)(2,1)}), bf16[8,2,2048]{2,1,0:T(2,128)(2,1)S(1)}, u32[]{:S(2)}, u32[]{:S(2)}) async-start(bf16[8,2,2048]{2,1,0:T(2,128)(2,1)} %reshape.150), calls=%async_computation | async-start | bytes 131072 | tf_op jit(solution)/shard_map/all_to_all | solution.py:118
  292.2 95.0 %reduce-scatter.3.cloned.1.call-start = ((), (), s32[]{:S(2)}) async-start(), calls=%async_computation.4 | async-start | bytes 946176 | tf_op jit(solution)/shard_map/reduce_scatter | solution.py:132
  307.5 5.5 %copy-start.2 = (f32[7168]{0:T(1024)S(1)}, f32[7168]{0:T(1024)}, u32[]{:S(2)}) copy-start(f32[7168]{0:T(1024)} %param.24) | copy-start | bytes 86020
  307.5 5.7 %copy-start.4 = (f32[64,2]{0,1:T(2,128)S(1)}, f32[64,2]{0,1:T(2,128)}, u32[]{:S(2)}) copy-start(f32[64,2]{0,1:T(2,128)} %param.26) | copy-start | bytes 1540
  307.5 5.7 %copy-start.5 = (s32[64,2]{0,1:T(2,128)S(1)}, s32[64,2]{0,1:T(2,128)}, u32[]{:S(2)}) copy-start(s32[64,2]{0,1:T(2,128)} %param.25) | copy-start | bytes 1540
  313.0 202.5 %reduce-scatter.5.cloned.1.call-start = ((), (), s32[]{:S(2)}) async-start(), calls=%async_computation.5 | async-start | bytes 946176 | tf_op jit(solution)/shard_map/reduce_scatter | solution.py:164
  313.3 73.8 %copy-start.3 = (bf16[8,1792]{1,0:T(8,128)(2,1)S(1)}, bf16[8,1792]{1,0:T(8,128)(2,1)}, u32[]{:S(2)}) copy-start(bf16[8,1792]{1,0:T(8,128)(2,1)} %param.16) | copy-start | bytes 86020
Sparse Core Ops, SparseCore 0:
  10.3 128.4 all-gather.2
  313.1 74.0 reduce-scatter.2
  441.8 73.6 reduce-scatter.4
where the time goes:
time: 528 us; the launch traced here: 523 us
  waiting for transfers between devices  266 us (50%)
  local copies, waits for them, and re-layouts  123 us (23%)
  matrix products  59.9 us (11%)
  blocking collectives  44.1 us (8%)
  between operations  13.9 us (3%)
  other arithmetic  11.5 us (2%)
    all_gather x1, waiting for transfers between devices, on_device(): lax.all_gather(prompt_latents, ('resp', 'expert'), axis=0, tiled=True)  125 us
    reduce_scatter x1, waiting for transfers between devices, on_device(): lax.psum_scatter(moe_terms.astype(jnp.bfloat16), ('resp', 'expert'), scat...  73.8 us
    reduce_scatter x1, waiting for transfers between devices, on_device(): lax.psum_scatter(out_terms.astype(jnp.bfloat16), ('resp', 'expert'), scat...  66.1 us
    all_gather x1, local copies, waits for them, and re-layouts, on_device(): lax.all_gather(prompt_latents, ('resp', 'expert'), axis=0, tiled=True)  51.6 us
    squeeze x32, local copies, waits for them, and re-layouts, fold_rows(): state, ignored = lax.scan(advance, state, blocks)  45.9 us
    all_gather x1, blocking collectives, on_device(): lax.all_gather(resid[None], ('resp', 'expert'), axis=0, tiled=True)  44.1 us
    dot_general x32, matrix products, online_step(): lax.dot_general(query_rows, block, (((1,), (1,)), ((), ())), preferred_el...  20.6 us
    dot_general x32, matrix products, online_step(): jnp.dot(weights.astype(jnp.bfloat16), block[:, :LAT], preferred_element_t...  18 us
  transfers between devices with their start and end apart: 4, of which 3 were waited for; matrix products, arithmetic and copies ran while one was open for 5% of the time, Pallas kernels for 0%

commit v1 on v0

v1 whole, which is shorter than its diff:
```python
import jax
import jax.numpy as jnp
from jax import lax
from jax.experimental import pallas as pl
from jax.experimental.pallas import tpu as pltpu
from jax.sharding import PartitionSpec as P

MESH = pl.DeviceIdType.MESH
BF = jnp.bfloat16
F32 = jnp.float32
LAT, ROPE, LATK = 512, 64, 576
SCALE2 = (128 + 64) ** -0.5 * 1.4426950408889634
FLOOR = -0.5e30
DEAD = -1e30
D = 7168
HALF = 896
KC = 256
GROUP = 512


def iota(shape, dim):
    return lax.broadcasted_iota(jnp.int32, shape, dim)


def dot(a, b):
    return jnp.dot(a, b, preferred_element_type=F32)


def kernel(
    slen,
    hid,
    newl,
    gain,
    gids,
    gwts,
    q_in,
    k_in,
    suf_in,
    vup_in,
    wo_in,
    wg_in,
    wu_in,
    wd_in,
    att_out,
    layer_out,
    q_all,
    qt,
    k_own,
    k_all,
    rope,
    kt_own,
    kt,
    suf,
    nl,
    acc,
    mx,
    sm,
    vup,
    wo,
    wg,
    wu,
    wd,
    ctx,
    hv,
    hv_tx,
    hv_rx,
    st_rx,
    a_buf,
    a_rx,
    a_sum,
    a_in,
    ag,
    m_buf,
    m_rx,
    m_sum,
    m_in,
    ld,
    kss,
    krs,
    rss,
    rrs,
    qss,
    qrs,
    qcs,
    qcr,
    hss,
    hrs,
    tss,
    trs,
    acs,
    acr,
    ars_s,
    ars_r,
    ags_s,
    ags_r,
    agc_s,
    agc_r,
    mcs,
    mcr,
    mrs_s,
    mrs_r,
):
    e = lax.axis_index("expert")
    r = lax.axis_index("resp")
    c = lax.rem(r, 2)
    z = r // 2
    right, left = lax.rem(e + 1, 4), lax.rem(e + 3, 4)
    twin = {"resp": z * 2 + 1 - c}

    def remote(src, dst, ssem, rsem, dev):
        return pltpu.make_async_remote_copy(
            src_ref=src, dst_ref=dst, send_sem=ssem, recv_sem=rsem, device_id=dev, device_id_type=MESH
        )

    def same_core(de, dz):
        return {"expert": lax.rem(e + de, 4), "resp": lax.rem(z + dz, 4) * 2 + c}

    loads = [
        pltpu.make_async_copy(q_in, q_all.at[r], ld.at[0]),
        pltpu.make_async_copy(k_in, k_own, ld.at[1]),
        pltpu.make_async_copy(suf_in, suf, ld.at[2]),
        pltpu.make_async_copy(vup_in, vup, ld.at[3]),
        pltpu.make_async_copy(wo_in, wo, ld.at[4]),
        pltpu.make_async_copy(wg_in, wg, ld.at[5]),
        pltpu.make_async_copy(wu_in, wu, ld.at[6]),
        pltpu.make_async_copy(wd_in, wd, ld.at[7]),
    ]
    for x in loads[:3]:
        x.start()

    bar = pltpu.get_barrier_semaphore()
    for i in range(1, 16):
        pl.semaphore_signal(bar, inc=1, device_id=same_core(i % 4, i // 4), device_id_type=MESH)
    for i in range(4):
        pl.semaphore_signal(
            bar,
            inc=1,
            device_id={"resp": lax.rem(z + i, 4) * 2 + 1 - c},
            device_id_type=MESH,
        )
    pl.semaphore_wait(bar, 19)

    def k_send(src, j, d):
        slot = 4 + 2 * j + d
        dev = {"expert": right if d == 0 else left}
        return remote(src, k_all.at[slot], kss.at[2 * j + d], krs.at[2 * j + d], dev)

    def rope_send(src, j, d):
        slot = 4 + 2 * j + d
        dev = {"expert": right if d == 0 else left}
        return remote(rope.at[src], rope.at[slot], rss.at[2 * j + d], rrs.at[2 * j + d], dev)

    def own_chunk(j, d):
        return j if d == 0 else 3 - j

    k_own_sends = [
        k_send(k_in.at[pl.ds(KC * own_chunk(j, d), KC), pl.ds(0, LAT)], j, d)
        for j in range(4)
        for d in range(2)
    ]
    rope_own_sends = [rope_send(own_chunk(j, d), j, d) for j in range(4) for d in range(2)]

    def q_send(i):
        return remote(q_in, q_all.at[r], qss.at[i], qrs.at[i], same_core(0, i))

    def q_cross(i):
        src = lax.rem(z + 4 - i, 4) * 2 + c
        return remote(q_all.at[src], q_all.at[src], qcs.at[i], qcr.at[i], twin)

    own_q_cross = remote(q_in, q_all.at[r], qcs.at[0], qcr.at[0], twin)
    own_q_cross.start()
    for x in k_own_sends[:2]:
        x.start()
    for i in (1, 3, 2):
        q_send(i).start()
    for x in k_own_sends[2:]:
        x.start()

    mx[...] = jnp.full_like(mx, FLOOR)
    sm[...] = jnp.zeros_like(sm)
    acc[...] = jnp.zeros_like(acc)
    nl[...] = jnp.zeros_like(nl)
    nl[0:8, :] = newl[...]

    loads[1].wait()
    rope_t = k_own[:, LAT:LATK].T
    for i in range(4):
        rope[i] = rope_t[:, KC * i : KC * (i + 1)]
    for x in rope_own_sends:
        x.start()
    for b in range(2):
        kt_own[b] = k_own[GROUP * b : GROUP * (b + 1), :LAT].T

    def soft(s, g, vt):
        old = mx[g]
        new = jnp.maximum(old, jnp.max(s, axis=0, keepdims=True))
        mx[g] = new
        p = jnp.exp2((s - new) * SCALE2)
        shrink = jnp.exp2((old - new) * SCALE2)
        sm[g] = sm[g] * shrink + jnp.sum(p, axis=0, keepdims=True)
        acc[g] = acc[g] * shrink + dot(vt, p.astype(BF))

    def make_qt(g):
        block = q_all[pl.ds(2 * g, 2)].reshape(GROUP, LATK)
        row, col = iota((GROUP, GROUP), 0), iota((GROUP, GROUP), 1)
        want = ((col // 8) % 2) * 256 + (col % 8) * 32 + col // 16
        place = jnp.where(row == want, 1.0, 0.0).astype(BF)
        qt[g] = dot(block.T, place).astype(BF)

    def own_keys(g):
        s0 = dot(k_own[0:GROUP, :], qt[g])
        s1 = dot(k_own[GROUP : 2 * GROUP, :], qt[g])
        soft(s0, g, kt_own[0])
        soft(s1, g, kt_own[1])

    loads[0].wait()
    own_q_cross.wait_recv()
    make_qt(z)
    loads[2].wait()
    for x in loads[3:]:
        x.start()
    tok = iota((1, GROUP), 1) % 16
    mine = (tok // 8) == c
    for b in range(2):
        rows = suf[GROUP * b : GROUP * (b + 1), :]
        s = dot(rows, qt[z])
        live = (iota((GROUP, GROUP), 0) < slen[b]) & mine & ((tok % 8) // 4 == b)
        kt[...] = rows[:, :LAT].T
        soft(jnp.where(live, s, DEAD), z, kt[...])
    s = dot(nl[...], qt[z])
    key = iota((128, GROUP), 0)
    live = (key < 8) & mine & ((tok % 8) // 4 == key // 4) & (key % 4 <= tok % 4)
    soft(jnp.where(live, s, DEAD), z, nl[:, :LAT].T)
    own_keys(z)

    for i in (1, 3, 2):
        q_send(i).wait_recv()
        q_cross(i).start()
    for i in (1, 3, 2):
        g = lax.rem(z + 4 - i, 4)
        q_cross(i).wait_recv()
        make_qt(g)
        own_keys(g)

    def pair(j, forward):
        for d in range(2):
            slot = 4 + 2 * j + d
            k_send(k_all.at[slot], j, d).wait_recv()
            rope_send(slot, j, d).wait_recv()
            if forward:
                k_send(k_all.at[slot], j + 4, d).start()
                rope_send(slot, j + 4, d).start()
        kn = k_all[pl.ds(4 + 2 * j, 2)].reshape(GROUP, LAT)
        rp = jnp.concatenate([rope[4 + 2 * j].T, rope[5 + 2 * j].T], axis=0)
        kt[...] = kn.T

        def score(g):
            return dot(kn, qt[g, 0:LAT, :]) + dot(rp, qt[g, LAT:LATK, :])

        s = score(0)
        for g in range(4):
            nxt = score(g + 1) if g < 3 else None
            soft(s, g, kt[...])
            s = nxt

    def pair_forward(j, carry):
        pair(j, True)
        return carry

    def pair_last(j, carry):
        pair(j, False)
        return carry

    lax.fori_loop(0, 2, pair_forward, 0)
    lax.fori_loop(2, 6, pair_last, 0)

    for g in range(4):
        part = (acc[g] * (1.0 / sm[g])).astype(BF)
        ctx[:, g] = part.T.reshape(32, 16, LAT)
    loads[3].wait()

    def project(h, carry):
        hv[h] = dot(ctx[h].reshape(64, LAT), vup[h]).reshape(4, 16, 128)
        return carry

    lax.fori_loop(0, 32, project, 0, unroll=4)
    for g in range(4):
        for hb in range(4):
            block = hv[8 * hb : 8 * hb + 8, g].reshape(128, 128).T.astype(BF)
            hv_tx[:, :, GROUP * g + 128 * hb : GROUP * g + 128 * hb + 128] = block.reshape(8, 16, 128)
        st_rx[0, 0:1, GROUP * g : GROUP * (g + 1)] = mx[g]
        st_rx[0, 1:2, GROUP * g : GROUP * (g + 1)] = sm[g]

    def hv_send(i):
        to = lax.rem(r + i, 8)
        return remote(hv_tx.at[to], hv_rx.at[i], hss.at[i], hrs.at[i], {"resp": to})

    def st_send(i):
        to = lax.rem(r + i, 8)
        return remote(st_rx.at[0], st_rx.at[i], tss.at[i], trs.at[i], {"resp": to})

    for i in range(1, 8):
        st_send(i).start()
        hv_send(i).start()
    for i in range(1, 8):
        st_send(i).wait_recv()
        hv_send(i).wait_recv()

    top = st_rx[0, 0:1, :]
    for i in range(1, 8):
        top = jnp.maximum(top, st_rx[i, 0:1, :])
    weights = []
    total = None
    for i in range(8):
        w = st_rx[i, 1:2, :] * jnp.exp2((st_rx[i, 0:1, :] - top) * SCALE2)
        weights.append(w)
        total = w if total is None else total + w
    inv = 1.0 / total
    y = hv_tx[r].astype(F32) * (weights[0] * inv)
    for i in range(1, 8):
        y = y + hv_rx[i].astype(F32) * (weights[i] * inv)
    y = y.astype(BF)

    col, row = iota((GROUP, 64), 1), iota((GROUP, 64), 0)
    want = ((row % 16) // 8) * 32 + (row // 128) * 8 + row % 8
    gather = jnp.where(col == want, 1.0, 0.0).astype(BF)
    keep = (iota((128, GROUP), 0) // 16) == ((iota((128, GROUP), 1) % 128) // 16)
    lhs = []
    for hb in range(4):
        piece = jnp.concatenate(
            [y[:, GROUP * g + 128 * hb : GROUP * g + 128 * hb + 128] for g in range(4)], axis=1
        )
        piece = jnp.concatenate([piece] * 8, axis=0)
        lhs.append(dot(jnp.where(keep, piece, jnp.zeros_like(piece)), gather))
    lhs = jnp.concatenate(lhs, axis=0).T.astype(BF)

    def core_send(buf, rx, ssem, rsem, x):
        return remote(buf.at[1 - c, x], rx.at[x], ssem.at[x], rsem.at[x], twin)

    def scatter_send(total_buf, landing, ssem, rsem, de, dz):
        src = total_buf.at[lax.rem(e + de, 4), lax.rem(z + dz, 4)]
        i = dz * 4 + de
        return remote(src, landing.at[i], ssem.at[i], rsem.at[i], same_core(de, dz))

    def fill(buf, x, tile):
        for cc in range(2):
            for g in range(4):
                rows = tile[32 * cc + 8 * g : 32 * cc + 8 * g + 8, :]
                buf[cc, x, g] = jnp.concatenate([rows[:, :HALF], rows[:, HALF:]], axis=0).astype(BF)

    def reduce_scatter(buf, rx, total_buf, landing, cs, cr, ss, sr):
        for de in (2, 1, 3, 0):
            x = lax.rem(e + de, 4)
            core_send(buf, rx, cs, cr, x).wait_recv()
            total_buf[x] = (buf[c, x].astype(F32) + rx[x].astype(F32)).astype(BF)
            for dz in (2, 1, 3, 0):
                if de or dz:
                    scatter_send(total_buf, landing, ss, sr, de, dz).start()
        out = total_buf[e, z].astype(F32)
        for dz in range(4):
            for de in range(4):
                if de or dz:
                    scatter_send(total_buf, landing, ss, sr, de, dz).wait_recv()
                    out = out + landing[dz * 4 + de].astype(F32)
        return out

    loads[4].wait()
    for x in range(4):
        fill(a_buf, x, dot(lhs, wo[:, 1792 * x : 1792 * (x + 1)]))
        core_send(a_buf, a_rx, acs, acr, x).start()
    attended = reduce_scatter(a_buf, a_rx, a_sum, a_in, acs, acr, ars_s, ars_r).astype(BF)
    hidden = jnp.concatenate([hid[:, :HALF], hid[:, HALF:]], axis=0)
    resid = (hidden.astype(F32) + attended.astype(F32)).astype(BF)
    ag[c, e, z] = resid
    att_out[...] = jnp.concatenate([attended[0:8], attended[8:16]], axis=1)

    def ag_send(de, dz):
        i = dz * 4 + de
        return remote(ag.at[c, e, z], ag.at[c, e, z], ags_s.at[i], ags_r.at[i], same_core(de, dz))

    def ag_cross(x):
        return remote(ag.at[c, x], ag.at[c, x], agc_s.at[x], agc_r.at[x], twin)

    for de in (0, 1, 3, 2):
        for dz in range(4):
            if de or dz:
                ag_send(de, dz).start()

    loads[5].wait()
    loads[6].wait()
    squares = jnp.zeros((64, 1), F32)
    gate = jnp.zeros((64, 256), F32)
    up = jnp.zeros((64, 256), F32)
    for de in (0, 1, 3, 2):
        x = lax.rem(e + 4 - de, 4)
        for dz in range(4):
            if de or dz:
                ag_send(de, dz).wait_recv()
        ag_cross(x).start()
    for de in (0, 1, 3, 2):
        x = lax.rem(e + 4 - de, 4)
        ag_cross(x).wait_recv()
        wide = ag[:, x].astype(F32)
        for half in range(2):
            part = wide[:, :, 8 * half : 8 * half + 8, :].reshape(64, HALF)
            squares = squares + jnp.sum(part * part, axis=1, keepdims=True)
            scaled = (part * gain[2 * x + half]).astype(BF)
            rows = pl.ds(pl.multiple_of(x * 1792 + half * HALF, HALF), HALF)
            gate = gate + dot(scaled, wg[rows, :])
            up = up + dot(scaled, wu[rows, :])
    norm = lax.rsqrt(squares * (1.0 / D) + 1e-6)
    gate = gate * norm
    up = up * norm
    act = (gate / (1.0 + jnp.exp(-gate)) * up).astype(BF)

    picked = jnp.where(gids[...] == e, gwts[...], 0.0)
    share = 2.5 * jnp.sum(picked, axis=1, keepdims=True) / jnp.sum(gwts[...], axis=1, keepdims=True)
    share = jnp.concatenate(
        [share[16 * g + 8 * cc : 16 * g + 8 * cc + 8] for cc in range(2) for g in range(4)], axis=0
    )
    loads[7].wait()
    for x in range(4):
        fill(m_buf, x, dot(act, wd[:, 1792 * x : 1792 * (x + 1)]) * share)
        core_send(m_buf, m_rx, mcs, mcr, x).start()
    moe = reduce_scatter(m_buf, m_rx, m_sum, m_in, mcs, mcr, mrs_s, mrs_r)
    out = (resid.astype(F32) + moe).astype(BF)
    layer_out[...] = jnp.concatenate([out[0:8], out[8:16]], axis=1)

    for x in k_own_sends + rope_own_sends:
        x.wait_send()
    for j in range(2):
        for d in range(2):
            slot = 4 + 2 * j + d
            k_send(k_all.at[slot], j + 4, d).wait_send()
            rope_send(slot, j + 4, d).wait_send()
    own_q_cross.wait_send()
    for i in range(1, 4):
        q_send(i).wait_send()
        q_cross(i).wait_send()
    for i in range(1, 8):
        hv_send(i).wait_send()
        st_send(i).wait_send()
    for x in range(4):
        core_send(a_buf, a_rx, acs, acr, x).wait_send()
        core_send(m_buf, m_rx, mcs, mcr, x).wait_send()
        ag_cross(x).wait_send()
    for i in range(1, 16):
        scatter_send(a_sum, a_in, ars_s, ars_r, i % 4, i // 4).wait_send()
        scatter_send(m_sum, m_in, mrs_s, mrs_r, i % 4, i // 4).wait_send()
        ag_send(i % 4, i // 4).wait_send()


def on_device(
    hidden,
    queries,
    new_latents,
    suffix_cache,
    suffix_lengths,
    prompt_latents,
    value_up,
    out_proj,
    rms_gain,
    gate_ids,
    gate_weights,
    w_gate,
    w_up,
    w_down,
):
    any_spec = pl.BlockSpec(memory_space=pl.ANY)
    vmem = pl.BlockSpec(memory_space=pltpu.VMEM)
    smem = pl.BlockSpec(memory_space=pltpu.SMEM)
    sem = pltpu.SemaphoreType.DMA
    out = jax.ShapeDtypeStruct((8, 1792), BF)
    block = (16, HALF)
    scratch = [
        pltpu.VMEM((8, 256, LATK), BF),
        pltpu.VMEM((4, LATK, GROUP), BF),
        pltpu.VMEM((1024, LATK), BF),
        pltpu.VMEM((16, KC, LAT), BF),
        pltpu.VMEM((16, ROPE, KC), BF),
        pltpu.VMEM((2, LAT, GROUP), BF),
        pltpu.VMEM((LAT, GROUP), BF),
        pltpu.VMEM((1024, LATK), BF),
        pltpu.VMEM((128, LATK), BF),
        pltpu.VMEM((4, LAT, GROUP), F32),
        pltpu.VMEM((4, 1, GROUP), F32),
        pltpu.VMEM((4, 1, GROUP), F32),
        pltpu.VMEM((32, LAT, 128), BF),
        pltpu.VMEM((512, D), BF),
        pltpu.VMEM((D, 256), BF),
        pltpu.VMEM((D, 256), BF),
        pltpu.VMEM((256, D), BF),
        pltpu.VMEM((32, 4, 16, LAT), BF),
        pltpu.VMEM((32, 4, 16, 128), F32),
        pltpu.VMEM((8, 16, 2048), BF),
        pltpu.VMEM((8, 16, 2048), BF),
        pltpu.VMEM((8, 2, 2048), F32),
        pltpu.VMEM((2, 4, 4) + block, BF),
        pltpu.VMEM((4, 4) + block, BF),
        pltpu.VMEM((4, 4) + block, BF),
        pltpu.VMEM((16,) + block, BF),
        pltpu.VMEM((2, 4, 4) + block, BF),
        pltpu.VMEM((2, 4, 4) + block, BF),
        pltpu.VMEM((4, 4) + block, BF),
        pltpu.VMEM((4, 4) + block, BF),
        pltpu.VMEM((16,) + block, BF),
    ] + [sem((n,)) for n in (8, 12, 12, 12, 12, 4, 4, 4, 4, 8, 8, 8, 8, 4, 4, 16, 16, 16, 16, 4, 4, 4, 4, 16, 16)]
    attended, layer = pl.pallas_call(
        kernel,
        out_shape=(out, out),
        in_specs=[smem] + [vmem] * 5 + [any_spec] * 8,
        out_specs=(vmem, vmem),
        scratch_shapes=scratch,
        compiler_params=pltpu.CompilerParams(
            collective_id=0, has_side_effects=True, vmem_limit_bytes=62 * 2**20
        ),
    )(
        suffix_lengths,
        hidden,
        new_latents,
        rms_gain.reshape(8, 1, HALF),
        gate_ids,
        gate_weights,
        queries.reshape(256, LATK),
        prompt_latents,
        suffix_cache.reshape(1024, LATK),
        value_up,
        out_proj.reshape(512, D),
        w_gate[0],
        w_up[0],
        w_down[0],
    )
    return attended, layer


def solution(mesh):
    placed = (
        P(("prompt", "resp"), "expert"),
        P(("prompt", "resp"), "expert", None),
        P(("prompt", "resp"), None),
        P(("prompt", "resp"), None, None),
        P(("prompt", "resp")),
        P(("prompt", "resp", "expert"), None),
        P("expert", None, None),
        P("expert", "resp", None),
        P(),
        P("prompt", None),
        P("prompt", None),
        P("expert", None, "resp"),
        P("expert", None, "resp"),
        P("expert", "resp", None),
    )
    return jax.shard_map(
        on_device,
        mesh=mesh,
        in_specs=placed,
        out_specs=(P(("prompt", "resp"), "expert"), P(("prompt", "resp"), "expert")),
        check_vma=False,
    )
```

time: 528 us -> 109 us (0.21)
  waiting for transfers between devices: 266 us -> 0 us
  local copies, waits for them, and re-layouts: 123 us -> 10.3 us
  Pallas kernels: 0 us -> 98 us
  matrix products: 59.9 us -> 0 us
  blocking collectives: 44.1 us -> 0 us
  between operations: 13.9 us -> 0.64 us
  other arithmetic: 11.5 us -> 0 us
    reduce_scatter x2 -> x0, waiting for transfers between devices: 140 us -> none  [the longest x1 73.8 us: on_device(): lax.psum_scatter(moe_terms.astype(jnp.bfloat16), ('resp', 'expert'), scat...]
    all_gather x1 -> x0, waiting for transfers between devices: 125 us -> none  [on_device(): lax.all_gather(prompt_latents, ('resp', 'expert'), axis=0, tiled=True)]
    pallas_call x0 -> x1, Pallas kernels: none -> 98 us  [on_device(): pl.pallas_call(kernel, out_shape=(out, out), in_specs=[smem] + [vmem] * 5...]
    dot_general x72 -> x0, matrix products: 59.9 us -> none  [the longest x32 20.6 us: online_step(): lax.dot_general(query_rows, block, (((1,), (1,)), ((), ())), preferred_el...]
    all_gather x1 -> x0, local copies, waits for them, and re-layouts: 51.6 us -> none  [on_device(): lax.all_gather(prompt_latents, ('resp', 'expert'), axis=0, tiled=True)]
    squeeze x32 -> x0, local copies, waits for them, and re-layouts: 45.9 us -> none  [fold_rows(): state, ignored = lax.scan(advance, state, blocks)]
    all_gather x1 -> x0, blocking collectives: 44.1 us -> none  [on_device(): lax.all_gather(resid[None], ('resp', 'expert'), axis=0, tiled=True)]
    reshape x3 -> x0, local copies, waits for them, and re-layouts: 15.6 us -> none  [the longest x1 14.1 us: on_device(): out_proj.reshape(out_proj.shape[0] * out_proj.shape[1], n_expert, out_pro...]
  transfers between devices with their start and end apart: 4 -> 0, of which waited for: 3 -> 0; matrix products, arithmetic and copies ran while one was open for 5% -> 0% of each run, Pallas kernels for 0% -> 0%
where the time goes in v1:
time: 109 us
  Pallas kernels  98 us (90%)
  local copies, waits for them, and re-layouts  10.3 us (9%)
    pallas_call x1, Pallas kernels, on_device(): pl.pallas_call(kernel, out_shape=(out, out), in_specs=[smem] + [vmem] * 5...  98 us
    unnamed x6, local copies, waits for them, and re-layouts  10.3 us

profile of v1, /device:TPU:1, one launch (start us, length us, event | category | flops | bytes accessed | tf_op | source)
XLA Modules:
  0.0 109.0 jit_solution(17654141860900855021)
XLA Ops:
  0.6 1.4 %copy.17.gids = s32[64,2]{1,0:T(8,128)} copy(s32[64,2]{0,1:T(2,128)} %param.23) | data formatting | bytes 1024 | tf_op args[9]
  2.0 1.4 %copy.18.gwts = f32[64,2]{1,0:T(8,128)} copy(f32[64,2]{0,1:T(2,128)} %param.24) | data formatting | bytes 1024 | tf_op args[10]
  3.4 2.4 %copy.16 = bf16[2,512,576]{2,1,0:T(8,128)(2,1)} copy(bf16[2,512,576]{1,2,0:T(8,128)(2,1)} %param.17) | data formatting | bytes 2359296 | tf_op args[3]
  5.8 2.4 %copy.19.k_in = bf16[1024,576]{1,0:T(8,128)(2,1)} copy(bf16[1024,576]{0,1:T(8,128)(2,1)} %param.19) | data formatting | bytes 2359296 | tf_op args[5]
  8.2 98.0 %shard_map.149 = (bf16[8,1792]{1,0:T(8,128)(2,1)}, bf16[8,1792]{1,0:T(8,128)(2,1)}) custom-call(s32[2]{0:T(128)} %slen.1, bf16[8,1792]{1,0:T(8,128)(2,1)} %hid.1, bf16[8,576]{1,0:T(8,128)(2,1)} %newl.1, f32[8,1,896]{2,1,0:T(1,128)} %bitcast.13, s32[64,2]{1,0:T(8,128)} %copy.17.gids, f32[64,2]{1,0:T(8,128)} %copy.18.gwts, bf16[256,576]{1,0:T(8,128)(2,1)} %bitcast.12, ...), custom_call_target="tpu_custom_call" | custom-call | tf_op jit(solution)/shard_map/pallas_call | solution.py:508
  106.2 1.4 %copy.22 = bf16[8,1792]{1,0:T(8,128)(2,1)} copy(bf16[8,1792]{1,0:T(8,128)(2,1)} %get-tuple-element.4) | data formatting | bytes 57344
  107.6 1.4 %copy.23 = bf16[8,1792]{1,0:T(8,128)(2,1)} copy(bf16[8,1792]{1,0:T(8,128)(2,1)} %get-tuple-element.5) | data formatting | bytes 57344

commit v2 on v1

v2 whole, which is shorter than its diff:
```python
import jax
import jax.numpy as jnp
from jax import lax
from jax.experimental import pallas as pl
from jax.experimental.pallas import tpu as pltpu
from jax.sharding import PartitionSpec as P

MESH = pl.DeviceIdType.MESH
BF = jnp.bfloat16
F32 = jnp.float32
LAT, ROPE, LATK = 512, 64, 576
SCALE2 = (128 + 64) ** -0.5 * 1.4426950408889634
FLOOR = -0.5e30
DEAD = -1e30
D = 7168
HALF = 896
KC = 256
GROUP = 512


def iota(shape, dim):
    return lax.broadcasted_iota(jnp.int32, shape, dim)


def dot(a, b):
    return jnp.dot(a, b, preferred_element_type=F32)


def kernel(
    slen,
    hid,
    newl,
    gain,
    gids,
    gwts,
    q_in,
    k_in,
    suf_in,
    vup_in,
    wo_in,
    wg_in,
    wu_in,
    wd_in,
    out_ref,
    q_own,
    q_all,
    place,
    qt,
    kt_own,
    kt_all,
    k_own,
    k_row,
    suf,
    nl,
    acc,
    mx,
    sm,
    vup,
    wo,
    wg,
    wu,
    wd,
    ctx,
    hv,
    hv_tx,
    hv_rx,
    st_rx,
    a_buf,
    a_rx,
    a_sum,
    a_in,
    ag,
    m_buf,
    m_rx,
    m_sum,
    m_in,
    ld,
    kss,
    krs,
    qss,
    qrs,
    qcs,
    qcr,
    near,
    far,
    hss,
    hrs,
    tss,
    trs,
    acs,
    acr,
    ars_s,
    ars_r,
    ags_s,
    ags_r,
    agc_s,
    agc_r,
    mcs,
    mcr,
    mrs_s,
    mrs_r,
):
    e = lax.axis_index("expert")
    r = lax.axis_index("resp")
    c = lax.rem(r, 2)
    z = r // 2
    right, left = lax.rem(e + 1, 4), lax.rem(e + 3, 4)
    twin = {"resp": z * 2 + 1 - c}

    def remote(src, dst, ssem, rsem, dev):
        return pltpu.make_async_remote_copy(
            src_ref=src, dst_ref=dst, send_sem=ssem, recv_sem=rsem, device_id=dev, device_id_type=MESH
        )

    def same_core(de, dz):
        return {"expert": lax.rem(e + de, 4), "resp": lax.rem(z + dz, 4) * 2 + c}

    loads = [
        pltpu.make_async_copy(q_in, q_own, ld.at[0]),
        pltpu.make_async_copy(k_in, kt_own, ld.at[1]),
        pltpu.make_async_copy(suf_in, suf, ld.at[2]),
        pltpu.make_async_copy(vup_in, vup, ld.at[3]),
        pltpu.make_async_copy(wo_in, wo, ld.at[4]),
        pltpu.make_async_copy(wg_in, wg, ld.at[5]),
        pltpu.make_async_copy(wu_in, wu, ld.at[6]),
        pltpu.make_async_copy(wd_in, wd, ld.at[7]),
    ]
    for x in loads[:3]:
        x.start()

    neighbours = [same_core(1, 0), same_core(3, 0), same_core(0, 1), same_core(0, 3), twin]
    bar = pltpu.get_barrier_semaphore()
    for x in neighbours:
        pl.semaphore_signal(bar, inc=1, device_id=x, device_id_type=MESH)
    loads[0].wait()
    q_all[r] = q_own[...].T
    pl.semaphore_wait(bar, 5)

    def k_send(src, j, d):
        dev = {"expert": right if d == 0 else left}
        return remote(src, kt_all.at[2 * j + d], kss.at[2 * j + d], krs.at[2 * j + d], dev)

    def own_chunk(j, d):
        return k_in.at[:, pl.ds(KC * (j if d == 0 else 3 - j), KC)]

    k_own_sends = [k_send(own_chunk(j, d), j, d) for j in range(4) for d in range(2)]

    def q_block(dz):
        return q_all.at[lax.rem(z + dz, 4) * 2 + c]

    half_rows = (pl.ds(0, LATK // 2), pl.ds(LATK // 2, LATK // 2))

    def q_send(i):
        if i < 2:
            part = q_block(0)
        else:
            part = q_block(3 if i == 2 else 1).at[half_rows[i - 2]]
        return remote(part, part, qss.at[i], qrs.at[i], same_core(0, 1 if i % 2 == 0 else 3))

    def q_come(i):
        if i < 2:
            part = q_block(3 if i == 0 else 1)
        else:
            part = q_block(2).at[half_rows[i - 2]]
        return remote(part, part, qss.at[i], qrs.at[i], same_core(0, 1 if i % 2 == 0 else 3))

    def q_cross(i):
        if i < 3:
            part = q_block((0, 3, 1)[i])
        else:
            part = q_block(2).at[half_rows[i - 3]]
        return remote(part, part, qcs.at[i], qcr.at[i], twin)

    def q_cross_come(i):
        if i < 3:
            part = q_all.at[lax.rem(z + (0, 3, 1)[i], 4) * 2 + 1 - c]
        else:
            part = q_all.at[lax.rem(z + 2, 4) * 2 + 1 - c].at[half_rows[i - 3]]
        return remote(part, part, qcs.at[i], qcr.at[i], twin)

    for x in k_own_sends[:2]:
        x.start()
    q_send(0).start()
    q_send(1).start()
    q_cross(0).start()
    for x in k_own_sends[2:]:
        x.start()
    for x in neighbours:
        pl.semaphore_signal(near, inc=1, device_id=x, device_id_type=MESH)

    mx[...] = jnp.full_like(mx, FLOOR)
    sm[...] = jnp.zeros_like(sm)
    acc[...] = jnp.zeros_like(acc)
    nl[...] = jnp.zeros_like(nl)
    nl[0:8, :] = newl[...]

    loads[1].wait()
    k_own[...] = kt_own[...].T

    def soft(s, g, vt):
        old = mx[g]
        new = jnp.maximum(old, jnp.max(s, axis=0, keepdims=True))
        mx[g] = new
        p = jnp.exp2((s - new) * SCALE2)
        shrink = jnp.exp2((old - new) * SCALE2)
        sm[g] = sm[g] * shrink + jnp.sum(p, axis=0, keepdims=True)
        acc[g] = acc[g] * shrink + dot(vt, p.astype(BF))

    row, col = iota((GROUP, GROUP), 0), iota((GROUP, GROUP), 1)
    want = ((col // 8) % 2) * 256 + (col % 8) * 32 + col // 16
    place[...] = jnp.where(row == want, 1.0, 0.0).astype(BF)

    def make_qt(g):
        block = jnp.concatenate([q_all[2 * g], q_all[2 * g + 1]], axis=1)
        qt[g] = dot(block, place[...]).astype(BF)

    def own_keys(g):
        s0 = dot(k_own[0:GROUP, :], qt[g])
        s1 = dot(k_own[GROUP : 2 * GROUP, :], qt[g])
        soft(s0, g, kt_own[0:LAT, 0:GROUP])
        soft(s1, g, kt_own[0:LAT, GROUP : 2 * GROUP])

    q_cross_come(0).wait_recv()
    make_qt(z)
    loads[2].wait()
    for x in loads[3:]:
        x.start()
    tok = iota((1, GROUP), 1) % 16
    mine = (tok // 8) == c
    for b in range(2):
        s = dot(suf[b].T, qt[z])
        live = (iota((GROUP, GROUP), 0) < slen[b]) & mine & ((tok % 8) // 4 == b)
        soft(jnp.where(live, s, DEAD), z, suf[b, 0:LAT, :])
    s = dot(nl[...], qt[z])
    key = iota((128, GROUP), 0)
    live = (key < 8) & mine & ((tok % 8) // 4 == key // 4) & (key % 4 <= tok % 4)
    soft(jnp.where(live, s, DEAD), z, nl[:, :LAT].T)
    own_keys(z)

    for i in range(2):
        q_come(i).wait_recv()
        q_cross(i + 1).start()
        q_send(i + 2).start()
    for i in range(2):
        g = lax.rem(z + (3, 1)[i], 4)
        q_cross_come(i + 1).wait_recv()
        make_qt(g)
        own_keys(g)
    for i in range(2):
        q_come(i + 2).wait_recv()
        q_cross(i + 3).start()
    for j in range(2):
        for d in range(2):
            k_send(kt_all.at[2 * j + d], j, d).wait_recv()
            k_send(kt_all.at[2 * j + d], j + 4, d).start()
    for i in range(2):
        q_cross_come(i + 3).wait_recv()
    make_qt(lax.rem(z + 2, 4))
    own_keys(lax.rem(z + 2, 4))
    pl.semaphore_wait(near, 5)
    for x in (same_core(2, 0), same_core(0, 2)):
        pl.semaphore_signal(far, inc=1, device_id=x, device_id_type=MESH)

    def arrive(j):
        for d in range(2):
            k_send(kt_all.at[2 * j + d], j, d).wait_recv()

    def pair(j):
        k_row[0:KC] = kt_all[2 * j].T
        k_row[KC : 2 * KC] = kt_all[2 * j + 1].T
        vt = jnp.concatenate([kt_all[2 * j, 0:LAT, :], kt_all[2 * j + 1, 0:LAT, :]], axis=1)

        s = dot(k_row[...], qt[0])
        for g in range(4):
            nxt = dot(k_row[...], qt[g + 1]) if g < 3 else None
            soft(s, g, vt)
            s = nxt

    def pair_last(j, carry):
        arrive(j)
        pair(j)
        return carry

    pair(0)
    pair(1)
    lax.fori_loop(2, 6, pair_last, 0)
    pl.semaphore_wait(far, 2)

    for g in range(4):
        part = (acc[g] * (1.0 / sm[g])).astype(BF)
        ctx[:, g] = part.T.reshape(32, 16, LAT)
    loads[3].wait()

    def project(h, carry):
        hv[h] = dot(ctx[h].reshape(64, LAT), vup[h]).reshape(4, 16, 128)
        return carry

    def hv_send(i, n):
        to = lax.rem(r + i, 8)
        return remote(hv_tx.at[n, to], hv_rx.at[n, i], hss.at[n, i], hrs.at[n, i], {"resp": to})

    def st_send(i):
        to = lax.rem(r + i, 8)
        return remote(st_rx.at[0], st_rx.at[i], tss.at[i], trs.at[i], {"resp": to})

    for g in range(4):
        for n in range(2):
            lanes = pl.ds(1024 * n + 256 * g, 256)
            st_rx[0, 0:1, lanes] = mx[g][:, 256 * n : 256 * n + 256]
            st_rx[0, 1:2, lanes] = sm[g][:, 256 * n : 256 * n + 256]
    for i in (4, 3, 5, 2, 6, 1, 7):
        st_send(i).start()
    for n in range(2):
        lax.fori_loop(16 * n, 16 * n + 16, project, 0, unroll=4)
        for g in range(4):
            for hb in range(2):
                first = 16 * n + 8 * hb
                block = hv[first : first + 8, g].reshape(128, 128).T.astype(BF)
                hv_tx[n, :, :, 256 * g + 128 * hb : 256 * g + 128 * hb + 128] = block.reshape(8, 16, 128)
        for i in (4, 3, 5, 2, 6, 1, 7):
            hv_send(i, n).start()

    for i in range(1, 8):
        st_send(i).wait_recv()
    top = st_rx[0, 0:1, :]
    for i in range(1, 8):
        top = jnp.maximum(top, st_rx[i, 0:1, :])
    weights = []
    total = None
    for i in range(8):
        w = st_rx[i, 1:2, :] * jnp.exp2((st_rx[i, 0:1, :] - top) * SCALE2)
        weights.append(w)
        total = w if total is None else total + w
    inv = 1.0 / total
    weights = [w * inv for w in weights]
    halves = []
    for n in range(2):
        lanes = slice(1024 * n, 1024 * n + 1024)
        y = hv_tx[n, r].astype(F32) * weights[0][:, lanes]
        for i in (4, 3, 5, 2, 6, 1, 7):
            hv_send(i, n).wait_recv()
            y = y + hv_rx[n, i].astype(F32) * weights[i][:, lanes]
        halves.append(y.astype(BF))

    col, row = iota((GROUP, 64), 1), iota((GROUP, 64), 0)
    want = ((row % 16) // 8) * 32 + (row // 128) * 8 + row % 8
    gather = jnp.where(col == want, 1.0, 0.0).astype(BF)
    keep = (iota((128, GROUP), 0) // 16) == ((iota((128, GROUP), 1) % 128) // 16)
    lhs = []
    for hb in range(4):
        piece = jnp.concatenate(
            [halves[hb // 2][:, 256 * g + 128 * (hb % 2) : 256 * g + 128 * (hb % 2) + 128] for g in range(4)],
            axis=1,
        )
        piece = jnp.concatenate([piece] * 8, axis=0)
        lhs.append(dot(jnp.where(keep, piece, jnp.zeros_like(piece)), gather))
    lhs = jnp.concatenate(lhs, axis=0).T.astype(BF)

    def core_send(buf, rx, ssem, rsem, x):
        return remote(buf.at[1 - c, x], rx.at[x], ssem.at[x], rsem.at[x], twin)

    def scatter_send(total_buf, landing, ssem, rsem, de, dz):
        src = total_buf.at[lax.rem(e + de, 4), lax.rem(z + dz, 4)]
        i = dz * 4 + de
        return remote(src, landing.at[i], ssem.at[i], rsem.at[i], same_core(de, dz))

    def fill(buf, x, tile):
        for cc in range(2):
            for g in range(4):
                rows = tile[32 * cc + 8 * g : 32 * cc + 8 * g + 8, :]
                buf[cc, x, g] = jnp.concatenate([rows[:, :HALF], rows[:, HALF:]], axis=0).astype(BF)

    def reduce_scatter(tile, buf, rx, total_buf, landing, cs, cr, ss, sr):
        def pass_on(de):
            x = lax.rem(e + de, 4)
            core_send(buf, rx, cs, cr, x).wait_recv()
            total_buf[x] = (buf[c, x].astype(F32) + rx[x].astype(F32)).astype(BF)
            for dz in (2, 1, 3, 0):
                if de or dz:
                    scatter_send(total_buf, landing, ss, sr, de, dz).start()

        last = None
        for de in (2, 1, 3, 0):
            x = lax.rem(e + de, 4)
            fill(buf, x, tile(x))
            core_send(buf, rx, cs, cr, x).start()
            if last is not None:
                pass_on(last)
            last = de
        pass_on(last)
        out = total_buf[e, z].astype(F32)
        for de in (2, 1, 3, 0):
            for dz in (2, 1, 3, 0):
                if de or dz:
                    scatter_send(total_buf, landing, ss, sr, de, dz).wait_recv()
                    out = out + landing[dz * 4 + de].astype(F32)
        return out

    def columns(x):
        return pl.ds(pl.multiple_of(x * 1792, 128), 1792)

    loads[4].wait()
    attended = reduce_scatter(
        lambda x: dot(lhs, wo[:, columns(x)]), a_buf, a_rx, a_sum, a_in, acs, acr, ars_s, ars_r
    ).astype(BF)
    hidden = jnp.concatenate([hid[:, :HALF], hid[:, HALF:]], axis=0)
    resid = (hidden.astype(F32) + attended.astype(F32)).astype(BF)
    ag[c, e, z] = resid
    out_ref[0] = jnp.concatenate([attended[0:8], attended[8:16]], axis=1)

    def ag_send(de, dz):
        i = dz * 4 + de
        return remote(ag.at[c, e, z], ag.at[c, e, z], ags_s.at[i], ags_r.at[i], same_core(de, dz))

    def ag_cross(x):
        return remote(ag.at[c, x], ag.at[c, x], agc_s.at[x], agc_r.at[x], twin)

    for de in (0, 1, 3, 2):
        for dz in range(4):
            if de or dz:
                ag_send(de, dz).start()

    loads[5].wait()
    loads[6].wait()
    squares = jnp.zeros((64, 1), F32)
    gate = jnp.zeros((64, 256), F32)
    up = jnp.zeros((64, 256), F32)
    def features(de, squares, gate, up):
        x = lax.rem(e + 4 - de, 4)
        ag_cross(x).wait_recv()
        wide = ag[:, x].astype(F32)
        for half in range(2):
            part = wide[:, :, 8 * half : 8 * half + 8, :].reshape(64, HALF)
            squares = squares + jnp.sum(part * part, axis=1, keepdims=True)
            scaled = (part * gain[2 * x + half]).astype(BF)
            rows = pl.ds(pl.multiple_of(x * 1792 + half * HALF, HALF), HALF)
            gate = gate + dot(scaled, wg[rows, :])
            up = up + dot(scaled, wu[rows, :])
        return squares, gate, up

    last = None
    for de in (0, 1, 3, 2):
        for dz in range(4):
            if de or dz:
                ag_send(de, dz).wait_recv()
        ag_cross(lax.rem(e + 4 - de, 4)).start()
        if last is not None:
            squares, gate, up = features(last, squares, gate, up)
        last = de
    squares, gate, up = features(last, squares, gate, up)
    norm = lax.rsqrt(squares * (1.0 / D) + 1e-6)
    gate = gate * norm
    up = up * norm
    act = (gate / (1.0 + jnp.exp(-gate)) * up).astype(BF)

    picked = jnp.where(gids[...] == e, gwts[...], 0.0)
    share = 2.5 * jnp.sum(picked, axis=0, keepdims=True) / jnp.sum(gwts[...], axis=0, keepdims=True)
    row, tok = iota((64, 64), 0), iota((64, 64), 1)
    here = tok == ((row // 8) % 4) * 16 + (row // 32) * 8 + row % 8
    share = jnp.sum(jnp.where(here, share, 0.0), axis=1, keepdims=True)
    loads[7].wait()
    moe = reduce_scatter(
        lambda x: dot(act, wd[:, columns(x)]) * share, m_buf, m_rx, m_sum, m_in, mcs, mcr, mrs_s, mrs_r
    )
    out = (resid.astype(F32) + moe).astype(BF)
    out_ref[1] = jnp.concatenate([out[0:8], out[8:16]], axis=1)

    for x in k_own_sends:
        x.wait_send()
    for j in range(2):
        for d in range(2):
            k_send(kt_all.at[2 * j + d], j + 4, d).wait_send()
    for i in range(4):
        q_send(i).wait_send()
    for i in range(5):
        q_cross(i).wait_send()
    for i in range(1, 8):
        st_send(i).wait_send()
        for n in range(2):
            hv_send(i, n).wait_send()
    for x in range(4):
        core_send(a_buf, a_rx, acs, acr, x).wait_send()
        core_send(m_buf, m_rx, mcs, mcr, x).wait_send()
        ag_cross(x).wait_send()
    for i in range(1, 16):
        scatter_send(a_sum, a_in, ars_s, ars_r, i % 4, i // 4).wait_send()
        scatter_send(m_sum, m_in, mrs_s, mrs_r, i % 4, i // 4).wait_send()
        ag_send(i % 4, i // 4).wait_send()


def on_device(
    hidden,
    queries,
    new_latents,
    suffix_cache,
    suffix_lengths,
    prompt_latents,
    value_up,
    out_proj,
    rms_gain,
    gate_ids,
    gate_weights,
    w_gate,
    w_up,
    w_down,
):
    any_spec = pl.BlockSpec(memory_space=pl.ANY)
    vmem = pl.BlockSpec(memory_space=pltpu.VMEM)
    smem = pl.BlockSpec(memory_space=pltpu.SMEM)
    sem = pltpu.SemaphoreType.DMA
    out = jax.ShapeDtypeStruct((2, 8, 1792), BF)
    block = (16, HALF)
    scratch = [
        pltpu.VMEM((256, LATK), BF),
        pltpu.VMEM((8, LATK, 256), BF),
        pltpu.VMEM((GROUP, GROUP), BF),
        pltpu.VMEM((4, LATK, GROUP), BF),
        pltpu.VMEM((LATK, 1024), BF),
        pltpu.VMEM((12, LATK, KC), BF),
        pltpu.VMEM((1024, LATK), BF),
        pltpu.VMEM((GROUP, LATK), BF),
        pltpu.VMEM((2, LATK, GROUP), BF),
        pltpu.VMEM((128, LATK), BF),
        pltpu.VMEM((4, LAT, GROUP), F32),
        pltpu.VMEM((4, 1, GROUP), F32),
        pltpu.VMEM((4, 1, GROUP), F32),
        pltpu.VMEM((32, LAT, 128), BF),
        pltpu.VMEM((512, D), BF),
        pltpu.VMEM((D, 256), BF),
        pltpu.VMEM((D, 256), BF),
        pltpu.VMEM((256, D), BF),
        pltpu.VMEM((32, 4, 16, LAT), BF),
        pltpu.VMEM((32, 4, 16, 128), F32),
        pltpu.VMEM((2, 8, 16, 1024), BF),
        pltpu.VMEM((2, 8, 16, 1024), BF),
        pltpu.VMEM((8, 2, 2048), F32),
        pltpu.VMEM((2, 4, 4) + block, BF),
        pltpu.VMEM((4, 4) + block, BF),
        pltpu.VMEM((4, 4) + block, BF),
        pltpu.VMEM((16,) + block, BF),
        pltpu.VMEM((2, 4, 4) + block, BF),
        pltpu.VMEM((2, 4, 4) + block, BF),
        pltpu.VMEM((4, 4) + block, BF),
        pltpu.VMEM((4, 4) + block, BF),
        pltpu.VMEM((16,) + block, BF),
    ]
    scratch += [sem((n,)) for n in (8, 12, 12, 4, 4, 5, 5)]
    scratch += [pltpu.SemaphoreType.REGULAR, pltpu.SemaphoreType.REGULAR]
    scratch += [sem((2, 8)), sem((2, 8))]
    scratch += [sem((n,)) for n in (8, 8, 4, 4, 16, 16, 16, 16, 4, 4, 4, 4, 16, 16)]
    both = pl.pallas_call(
        kernel,
        out_shape=out,
        in_specs=[smem] + [vmem] * 5 + [any_spec] * 8,
        out_specs=vmem,
        scratch_shapes=scratch,
        compiler_params=pltpu.CompilerParams(
            collective_id=0, has_side_effects=True, vmem_limit_bytes=62 * 2**20
        ),
    )(
        suffix_lengths,
        hidden,
        new_latents,
        rms_gain.reshape(8, 1, HALF),
        gate_ids.T,
        gate_weights.T,
        queries.reshape(256, LATK),
        prompt_latents.T,
        jnp.swapaxes(suffix_cache, 1, 2),
        value_up,
        out_proj.reshape(512, D),
        w_gate[0],
        w_up[0],
        w_down[0],
    )
    return both[0], both[1]


def solution(mesh):
    placed = (
        P(("prompt", "resp"), "expert"),
        P(("prompt", "resp"), "expert", None),
        P(("prompt", "resp"), None),
        P(("prompt", "resp"), None, None),
        P(("prompt", "resp")),
        P(("prompt", "resp", "expert"), None),
        P("expert", None, None),
        P("expert", "resp", None),
        P(),
        P("prompt", None),
        P("prompt", None),
        P("expert", None, "resp"),
        P("expert", None, "resp"),
        P("expert", "resp", None),
    )
    return jax.shard_map(
        on_device,
        mesh=mesh,
        in_specs=placed,
        out_specs=(P(("prompt", "resp"), "expert"), P(("prompt", "resp"), "expert")),
        check_vma=False,
    )
```

time: 109 us -> 95.2 us (0.87)
  local copies, waits for them, and re-layouts: 10.3 us -> 1.39 us
  Pallas kernels: 98 us -> 92.9 us
    unnamed x6 -> x0, local copies, waits for them, and re-layouts: 10.3 us -> none
    pallas_call x1, Pallas kernels: 98 us -> 92.9 us  [on_device(): pl.pallas_call(kernel, out_shape=out, in_specs=[smem] + [vmem] * 5 + [any...]
    squeeze x0 -> x1, local copies, waits for them, and re-layouts: none -> 1.39 us  [on_device(): return (both[0], both[1])]
where the time goes in v2:
time: 95.2 us; the launch traced here: 95 us
  Pallas kernels  92.9 us (98%)
  local copies, waits for them, and re-layouts  1.39 us (1%)
    pallas_call x1, Pallas kernels, on_device(): pl.pallas_call(kernel, out_shape=out, in_specs=[smem] + [vmem] * 5 + [any...  92.9 us

profile of v2, /device:TPU:1, one launch (start us, length us, event | category | flops | bytes accessed | tf_op | source)
XLA Modules:
  0.0 95.0 jit_solution(14062216571724744996)
XLA Ops:
  0.6 92.9 %shard_map.149 = bf16[2,8,1792]{2,1,0:T(8,128)(2,1)} custom-call(s32[2]{0:T(128)} %slen.1, bf16[8,1792]{1,0:T(8,128)(2,1)} %hid.1, bf16[8,576]{1,0:T(8,128)(2,1)} %newl.1, f32[8,1,896]{2,1,0:T(1,128)} %bitcast.21, s32[2,64]{1,0:T(2,128)} %bitcast.22, f32[2,64]{1,0:T(2,128)} %bitcast.23, bf16[256,576]{1,0:T(8,128)(2,1)} %bitcast.20, ...), custom_call_target="tpu_custom_call" | custom-call | tf_op jit(solution)/shard_map/pallas_call | solution.py:551
  93.6 1.4 %slice_bitcast_fusion = (bf16[8,1792]{1,0:T(8,128)(2,1)}, bf16[8,1792]{1,0:T(8,128)(2,1)}) fusion(bf16[2,8,1792]{2,1,0:T(8,128)(2,1)} %shard_map.149), kind=kLoop, calls=%fused_computation | loop fusion | bytes 114688 | tf_op jit(solution)/shard_map/squeeze | solution.py:576

commit v3 on v2

--- a/solution.py
+++ b/solution.py
@@ -63,8 +63,12 @@
     ctx,
     hv,
     hv_tx,
-    hv_rx,
-    st_rx,
+    hv_tw,
+    st_own,
+    st_tw,
+    z_tx,
+    z_rx,
+    st_z,
     a_buf,
     a_rx,
     a_sum,
@@ -83,10 +87,14 @@
     qcr,
     near,
     far,
-    hss,
-    hrs,
+    tws,
+    twr,
     tss,
-    trs,
+    tsr,
+    zss,
+    zrs,
+    zts,
+    ztr,
     acs,
     acr,
     ars_s,
@@ -143,6 +151,22 @@
     def own_chunk(j, d):
         return k_in.at[:, pl.ds(KC * (j if d == 0 else 3 - j), KC)]
 
+    def k_forward(j, d):
+        dev = {"expert": right if d == 0 else left}
+        if j == 0:
+            return [k_send(kt_all.at[d], 4, d)]
+        sems = (10 + d, 12 + d)
+        return [
+            remote(
+                kt_all.at[2 + d, :, pl.ds(128 * i, 128)],
+                kt_all.at[10 + d, :, pl.ds(128 * i, 128)],
+                kss.at[sems[i]],
+                krs.at[sems[i]],
+                dev,
+            )
+            for i in range(2)
+        ]
+
     k_own_sends = [k_send(own_chunk(j, d), j, d) for j in range(4) for d in range(2)]
 
     def q_block(dz):
@@ -252,7 +276,8 @@
     for j in range(2):
         for d in range(2):
             k_send(kt_all.at[2 * j + d], j, d).wait_recv()
-            k_send(kt_all.at[2 * j + d], j + 4, d).start()
+            for x in k_forward(j, d):
+                x.start()
     for i in range(2):
         q_cross_come(i + 3).wait_recv()
     make_qt(lax.rem(z + 2, 4))
@@ -265,16 +290,23 @@
         for d in range(2):
             k_send(kt_all.at[2 * j + d], j, d).wait_recv()
 
-    def pair(j):
-        k_row[0:KC] = kt_all[2 * j].T
-        k_row[KC : 2 * KC] = kt_all[2 * j + 1].T
-        vt = jnp.concatenate([kt_all[2 * j, 0:LAT, :], kt_all[2 * j + 1, 0:LAT, :]], axis=1)
-
-        s = dot(k_row[...], qt[0])
+    def keys_of(pieces):
+        at = 0
+        for slot, first, width in pieces:
+            k_row[at : at + width] = kt_all[slot, :, first : first + width].T
+            at += width
+        return jnp.concatenate([kt_all[slot, 0:LAT, first : first + width] for slot, first, width in pieces], axis=1)
+
+    def groups(count, vt):
+        s = dot(k_row[0:count], qt[0])
         for g in range(4):
-            nxt = dot(k_row[...], qt[g + 1]) if g < 3 else None
+            nxt = dot(k_row[0:count], qt[g + 1]) if g < 3 else None
             soft(s, g, vt)
             s = nxt
+
+    def pair(j):
+        vt = keys_of([(2 * j, 0, KC), (2 * j + 1, 0, KC)])
+        groups(GROUP, vt)
 
     def pair_last(j, carry):
         arrive(j)
@@ -283,64 +315,93 @@
 
     pair(0)
     pair(1)
-    lax.fori_loop(2, 6, pair_last, 0)
+    lax.fori_loop(2, 5, pair_last, 0)
+    for d in range(2):
+        k_forward(1, d)[0].wait_recv()
+    groups(KC, keys_of([(10, 0, 128), (11, 0, 128)]))
     pl.semaphore_wait(far, 2)
-
-    for g in range(4):
-        part = (acc[g] * (1.0 / sm[g])).astype(BF)
-        ctx[:, g] = part.T.reshape(32, 16, LAT)
     loads[3].wait()
-
-    def project(h, carry):
-        hv[h] = dot(ctx[h].reshape(64, LAT), vup[h]).reshape(4, 16, 128)
-        return carry
-
-    def hv_send(i, n):
-        to = lax.rem(r + i, 8)
-        return remote(hv_tx.at[n, to], hv_rx.at[n, i], hss.at[n, i], hrs.at[n, i], {"resp": to})
-
-    def st_send(i):
-        to = lax.rem(r + i, 8)
-        return remote(st_rx.at[0], st_rx.at[i], tss.at[i], trs.at[i], {"resp": to})
-
-    for g in range(4):
-        for n in range(2):
-            lanes = pl.ds(1024 * n + 256 * g, 256)
-            st_rx[0, 0:1, lanes] = mx[g][:, 256 * n : 256 * n + 256]
-            st_rx[0, 1:2, lanes] = sm[g][:, 256 * n : 256 * n + 256]
-    for i in (4, 3, 5, 2, 6, 1, 7):
-        st_send(i).start()
-    for n in range(2):
-        lax.fori_loop(16 * n, 16 * n + 16, project, 0, unroll=4)
+    for d in range(2):
+        k_forward(1, d)[1].wait_recv()
+    vt = keys_of([(10, 128, 128), (11, 128, 128)])
+
+    def lanes_of(ref, q):
+        return jnp.concatenate([ref[g, :, 128 * q : 128 * q + 128] for g in range(4)], axis=1)
+
+    def last_scores(q):
+        return dot(k_row[0:KC], lanes_of(qt, q))
+
+    def finish(q, s):
+        old = lanes_of(mx, q)
+        new = jnp.maximum(old, jnp.max(s, axis=0, keepdims=True))
+        p = jnp.exp2((s - new) * SCALE2)
+        shrink = jnp.exp2((old - new) * SCALE2)
+        total = lanes_of(sm, q) * shrink + jnp.sum(p, axis=0, keepdims=True)
+        part = (lanes_of(acc, q) * shrink + dot(vt, p.astype(BF))) * (1.0 / total)
+        st_own[q, 0:1, :] = new
+        st_own[q, 1:2, :] = total
+        ctx[q] = part.astype(BF).T.reshape(4, 8, 16, LAT)
+        for h in range(8):
+            hv[8 * q + h] = dot(ctx[q, :, h].reshape(64, LAT), vup[8 * q + h]).reshape(4, 16, 128)
         for g in range(4):
-            for hb in range(2):
-                first = 16 * n + 8 * hb
-                block = hv[first : first + 8, g].reshape(128, 128).T.astype(BF)
-                hv_tx[n, :, :, 256 * g + 128 * hb : 256 * g + 128 * hb + 128] = block.reshape(8, 16, 128)
-        for i in (4, 3, 5, 2, 6, 1, 7):
-            hv_send(i, n).start()
-
-    for i in range(1, 8):
-        st_send(i).wait_recv()
-    top = st_rx[0, 0:1, :]
-    for i in range(1, 8):
-        top = jnp.maximum(top, st_rx[i, 0:1, :])
-    weights = []
-    total = None
-    for i in range(8):
-        w = st_rx[i, 1:2, :] * jnp.exp2((st_rx[i, 0:1, :] - top) * SCALE2)
-        weights.append(w)
-        total = w if total is None else total + w
-    inv = 1.0 / total
-    weights = [w * inv for w in weights]
-    halves = []
-    for n in range(2):
-        lanes = slice(1024 * n, 1024 * n + 1024)
-        y = hv_tx[n, r].astype(F32) * weights[0][:, lanes]
-        for i in (4, 3, 5, 2, 6, 1, 7):
-            hv_send(i, n).wait_recv()
-            y = y + hv_rx[n, i].astype(F32) * weights[i][:, lanes]
-        halves.append(y.astype(BF))
+            block = hv[8 * q : 8 * q + 8, g].reshape(128, 128).T.astype(BF).reshape(4, 2, 16, 128)
+            for cc in range(2):
+                hv_tx[q, cc, :, :, 128 * g : 128 * g + 128] = block[:, cc]
+
+    def twin_sends(q):
+        return [
+            remote(hv_tx.at[q, 1 - c], hv_tw.at[q], tws.at[q], twr.at[q], twin),
+            remote(st_own.at[q], st_tw.at[q], tss.at[q], tsr.at[q], twin),
+        ]
+
+    def z_sends(q, dz):
+        to = lax.rem(z + dz, 4)
+        dev = same_core(0, dz)
+        return [
+            remote(z_tx.at[q, to], z_rx.at[q, dz], zss.at[q, dz], zrs.at[q, dz], dev),
+            remote(st_z.at[q, 0], st_z.at[q, dz], zts.at[q, dz], ztr.at[q, dz], dev),
+        ]
+
+    def weight(st, top):
+        return st[1:2, :] * jnp.exp2((st[0:1, :] - top) * SCALE2)
+
+    def chip_sum(q):
+        for x in twin_sends(q):
+            x.wait_recv()
+        top = jnp.maximum(st_own[q, 0:1, :], st_tw[q, 0:1, :])
+        w1, w2 = weight(st_own[q], top), weight(st_tw[q], top)
+        inv = 1.0 / (w1 + w2)
+        mine = hv_tx[q, c].astype(F32) * (w1 * inv) + hv_tw[q].astype(F32) * (w2 * inv)
+        z_tx[q] = mine.astype(BF)
+        st_z[q, 0, 0:1, :] = top
+        st_z[q, 0, 1:2, :] = w1 + w2
+        for dz in (2, 1, 3):
+            for x in z_sends(q, dz):
+                x.start()
+
+    def plane_sum(q):
+        for dz in (2, 1, 3):
+            for x in z_sends(q, dz):
+                x.wait_recv()
+        top = st_z[q, 0, 0:1, :]
+        for dz in range(1, 4):
+            top = jnp.maximum(top, st_z[q, dz, 0:1, :])
+        w = [weight(st_z[q, dz], top) for dz in range(4)]
+        y = z_tx[q, z].astype(F32) * w[0]
+        for dz in range(1, 4):
+            y = y + z_rx[q, dz].astype(F32) * w[dz]
+        return (y * (1.0 / (w[0] + w[1] + w[2] + w[3]))).astype(BF)
+
+    s = last_scores(0)
+    for q in range(4):
+        nxt = last_scores(q + 1) if q < 3 else None
+        finish(q, s)
+        for x in twin_sends(q):
+            x.start()
+        if q > 0:
+            chip_sum(q - 1)
+        s = nxt
+    chip_sum(3)
 
     col, row = iota((GROUP, 64), 1), iota((GROUP, 64), 0)
     want = ((row % 16) // 8) * 32 + (row // 128) * 8 + row % 8
@@ -348,10 +409,7 @@
     keep = (iota((128, GROUP), 0) // 16) == ((iota((128, GROUP), 1) % 128) // 16)
     lhs = []
     for hb in range(4):
-        piece = jnp.concatenate(
-            [halves[hb // 2][:, 256 * g + 128 * (hb % 2) : 256 * g + 128 * (hb % 2) + 128] for g in range(4)],
-            axis=1,
-        )
+        piece = plane_sum(hb)
         piece = jnp.concatenate([piece] * 8, axis=0)
         lhs.append(dot(jnp.where(keep, piece, jnp.zeros_like(piece)), gather))
     lhs = jnp.concatenate(lhs, axis=0).T.astype(BF)
@@ -469,15 +527,18 @@
         x.wait_send()
     for j in range(2):
         for d in range(2):
-            k_send(kt_all.at[2 * j + d], j + 4, d).wait_send()
+            for x in k_forward(j, d):
+                x.wait_send()
     for i in range(4):
         q_send(i).wait_send()
     for i in range(5):
         q_cross(i).wait_send()
-    for i in range(1, 8):
-        st_send(i).wait_send()
-        for n in range(2):
-            hv_send(i, n).wait_send()
+    for q in range(4):
+        for x in twin_sends(q):
+            x.wait_send()
+        for dz in range(1, 4):
+            for x in z_sends(q, dz):
+                x.wait_send()
     for x in range(4):
         core_send(a_buf, a_rx, acs, acr, x).wait_send()
         core_send(m_buf, m_rx, mcs, mcr, x).wait_send()
@@ -529,11 +590,15 @@
         pltpu.VMEM((D, 256), BF),
         pltpu.VMEM((D, 256), BF),
         pltpu.VMEM((256, D), BF),
-        pltpu.VMEM((32, 4, 16, LAT), BF),
+        pltpu.VMEM((4, 4, 8, 16, LAT), BF),
         pltpu.VMEM((32, 4, 16, 128), F32),
-        pltpu.VMEM((2, 8, 16, 1024), BF),
-        pltpu.VMEM((2, 8, 16, 1024), BF),
-        pltpu.VMEM((8, 2, 2048), F32),
+        pltpu.VMEM((4, 2, 4, 16, GROUP), BF),
+        pltpu.VMEM((4, 4, 16, GROUP), BF),
+        pltpu.VMEM((4, 2, GROUP), F32),
+        pltpu.VMEM((4, 2, GROUP), F32),
+        pltpu.VMEM((4, 4, 16, GROUP), BF),
+        pltpu.VMEM((4, 4, 16, GROUP), BF),
+        pltpu.VMEM((4, 4, 2, GROUP), F32),
         pltpu.VMEM((2, 4, 4) + block, BF),
         pltpu.VMEM((4, 4) + block, BF),
         pltpu.VMEM((4, 4) + block, BF),
@@ -544,10 +609,10 @@
         pltpu.VMEM((4, 4) + block, BF),
         pltpu.VMEM((16,) + block, BF),
     ]
-    scratch += [sem((n,)) for n in (8, 12, 12, 4, 4, 5, 5)]
+    scratch += [sem((n,)) for n in (8, 14, 14, 4, 4, 5, 5)]
     scratch += [pltpu.SemaphoreType.REGULAR, pltpu.SemaphoreType.REGULAR]
-    scratch += [sem((2, 8)), sem((2, 8))]
-    scratch += [sem((n,)) for n in (8, 8, 4, 4, 16, 16, 16, 16, 4, 4, 4, 4, 16, 16)]
+    scratch += [sem((4,))] * 4 + [sem((4, 4))] * 4
+    scratch += [sem((n,)) for n in (4, 4, 16, 16, 16, 16, 4, 4, 4, 4, 16, 16)]
     both = pl.pallas_call(
         kernel,
         out_shape=out,

time: 95.2 us -> 92.4 us (0.971)
  Pallas kernels: 92.9 us -> 90.1 us
    pallas_call x1, Pallas kernels: 92.9 us -> 90.1 us  [on_device(): pl.pallas_call(kernel, out_shape=out, in_specs=[smem] + [vmem] * 5 + [any...]
where the time goes in v3:
time: 92.4 us; the launch traced here: 92.1 us
  Pallas kernels  90.1 us (98%)
  local copies, waits for them, and re-layouts  1.39 us (2%)
    pallas_call x1, Pallas kernels, on_device(): pl.pallas_call(kernel, out_shape=out, in_specs=[smem] + [vmem] * 5 + [any...  90.1 us

profile of v3, /device:TPU:1, one launch (start us, length us, event | category | flops | bytes accessed | tf_op | source)
XLA Modules:
  0.0 92.1 jit_solution(6379863594234727330)
XLA Ops:
  0.6 90.1 %shard_map.149 = bf16[2,8,1792]{2,1,0:T(8,128)(2,1)} custom-call(s32[2]{0:T(128)} %slen.1, bf16[8,1792]{1,0:T(8,128)(2,1)} %hid.1, bf16[8,576]{1,0:T(8,128)(2,1)} %newl.1, f32[8,1,896]{2,1,0:T(1,128)} %bitcast.21, s32[2,64]{1,0:T(2,128)} %bitcast.22, f32[2,64]{1,0:T(2,128)} %bitcast.23, bf16[256,576]{1,0:T(8,128)(2,1)} %bitcast.20, ...), custom_call_target="tpu_custom_call" | custom-call | tf_op jit(solution)/shard_map/pallas_call | solution.py:616
  90.8 1.4 %slice_bitcast_fusion = (bf16[8,1792]{1,0:T(8,128)(2,1)}, bf16[8,1792]{1,0:T(8,128)(2,1)}) fusion(bf16[2,8,1792]{2,1,0:T(8,128)(2,1)} %shard_map.149), kind=kLoop, calls=%fused_computation | loop fusion | bytes 114688 | tf_op jit(solution)/shard_map/squeeze | solution.py:641

commit v4 on v3

--- a/solution.py
+++ b/solution.py
@@ -422,30 +422,30 @@
         i = dz * 4 + de
         return remote(src, landing.at[i], ssem.at[i], rsem.at[i], same_core(de, dz))
 
-    def fill(buf, x, tile):
-        for cc in range(2):
-            for g in range(4):
-                rows = tile[32 * cc + 8 * g : 32 * cc + 8 * g + 8, :]
-                buf[cc, x, g] = jnp.concatenate([rows[:, :HALF], rows[:, HALF:]], axis=0).astype(BF)
-
-    def reduce_scatter(tile, buf, rx, total_buf, landing, cs, cr, ss, sr):
-        def pass_on(de):
-            x = lax.rem(e + de, 4)
-            core_send(buf, rx, cs, cr, x).wait_recv()
-            total_buf[x] = (buf[c, x].astype(F32) + rx[x].astype(F32)).astype(BF)
-            for dz in (2, 1, 3, 0):
-                if de or dz:
-                    scatter_send(total_buf, landing, ss, sr, de, dz).start()
-
-        last = None
+    def shares(h, tile, buf, rx, cs, cr):
         for de in (2, 1, 3, 0):
             x = lax.rem(e + de, 4)
-            fill(buf, x, tile(x))
-            core_send(buf, rx, cs, cr, x).start()
-            if last is not None:
-                pass_on(last)
-            last = de
-        pass_on(last)
+            terms = tile(x)
+            for g in range(4):
+                rows = terms[8 * g : 8 * g + 8, :]
+                buf[h, x, g] = jnp.concatenate([rows[:, :HALF], rows[:, HALF:]], axis=0).astype(BF)
+
+            @pl.when(c != h)
+            def _():
+                core_send(buf, rx, cs, cr, x).start()
+
+    def pass_on(h, buf, rx, total_buf, landing, cs, cr, ss, sr):
+        @pl.when(c == h)
+        def _():
+            for de in (2, 1, 3, 0):
+                x = lax.rem(e + de, 4)
+                core_send(buf, rx, cs, cr, x).wait_recv()
+                total_buf[x] = (buf[h, x].astype(F32) + rx[x].astype(F32)).astype(BF)
+                for dz in (2, 1, 3, 0):
+                    if de or dz:
+                        scatter_send(total_buf, landing, ss, sr, de, dz).start()
+
+    def collect(total_buf, landing, ss, sr):
         out = total_buf[e, z].astype(F32)
         for de in (2, 1, 3, 0):
             for dz in (2, 1, 3, 0):
@@ -458,13 +458,9 @@
         return pl.ds(pl.multiple_of(x * 1792, 128), 1792)
 
     loads[4].wait()
-    attended = reduce_scatter(
-        lambda x: dot(lhs, wo[:, columns(x)]), a_buf, a_rx, a_sum, a_in, acs, acr, ars_s, ars_r
-    ).astype(BF)
-    hidden = jnp.concatenate([hid[:, :HALF], hid[:, HALF:]], axis=0)
-    resid = (hidden.astype(F32) + attended.astype(F32)).astype(BF)
-    ag[c, e, z] = resid
-    out_ref[0] = jnp.concatenate([attended[0:8], attended[8:16]], axis=1)
+    for h in range(2):
+        shares(h, lambda x: dot(lhs[32 * h : 32 * h + 32], wo[:, columns(x)]), a_buf, a_rx, acs, acr)
+        pass_on(h, a_buf, a_rx, a_sum, a_in, acs, acr, ars_s, ars_r)
 
     def ag_send(de, dz):
         i = dz * 4 + de
@@ -473,54 +469,71 @@
     def ag_cross(x):
         return remote(ag.at[c, x], ag.at[c, x], agc_s.at[x], agc_r.at[x], twin)
 
-    for de in (0, 1, 3, 2):
-        for dz in range(4):
-            if de or dz:
-                ag_send(de, dz).start()
-
-    loads[5].wait()
-    loads[6].wait()
-    squares = jnp.zeros((64, 1), F32)
-    gate = jnp.zeros((64, 256), F32)
-    up = jnp.zeros((64, 256), F32)
-    def features(de, squares, gate, up):
-        x = lax.rem(e + 4 - de, 4)
-        ag_cross(x).wait_recv()
-        wide = ag[:, x].astype(F32)
-        for half in range(2):
-            part = wide[:, :, 8 * half : 8 * half + 8, :].reshape(64, HALF)
-            squares = squares + jnp.sum(part * part, axis=1, keepdims=True)
-            scaled = (part * gain[2 * x + half]).astype(BF)
-            rows = pl.ds(pl.multiple_of(x * 1792 + half * HALF, HALF), HALF)
-            gate = gate + dot(scaled, wg[rows, :])
-            up = up + dot(scaled, wu[rows, :])
-        return squares, gate, up
-
-    last = None
-    for de in (0, 1, 3, 2):
-        for dz in range(4):
-            if de or dz:
-                ag_send(de, dz).wait_recv()
-        ag_cross(lax.rem(e + 4 - de, 4)).start()
-        if last is not None:
-            squares, gate, up = features(last, squares, gate, up)
-        last = de
-    squares, gate, up = features(last, squares, gate, up)
-    norm = lax.rsqrt(squares * (1.0 / D) + 1e-6)
-    gate = gate * norm
-    up = up * norm
-    act = (gate / (1.0 + jnp.exp(-gate)) * up).astype(BF)
+    def ag_cross_come(x):
+        return remote(ag.at[1 - c, x], ag.at[1 - c, x], agc_s.at[x], agc_r.at[x], twin)
+
+    def residual(h):
+        @pl.when(c == h)
+        def _():
+            attended = collect(a_sum, a_in, ars_s, ars_r).astype(BF)
+            hidden = jnp.concatenate([hid[:, :HALF], hid[:, HALF:]], axis=0)
+            ag[h, e, z] = (hidden.astype(F32) + attended.astype(F32)).astype(BF)
+            for de in (0, 1, 3, 2):
+                for dz in range(4):
+                    if de or dz:
+                        ag_send(de, dz).start()
+            out_ref[0] = jnp.concatenate([attended[0:8], attended[8:16]], axis=1)
+
+    residual(0)
+    residual(1)
 
     picked = jnp.where(gids[...] == e, gwts[...], 0.0)
     share = 2.5 * jnp.sum(picked, axis=0, keepdims=True) / jnp.sum(gwts[...], axis=0, keepdims=True)
     row, tok = iota((64, 64), 0), iota((64, 64), 1)
     here = tok == ((row // 8) % 4) * 16 + (row // 32) * 8 + row % 8
     share = jnp.sum(jnp.where(here, share, 0.0), axis=1, keepdims=True)
+    loads[5].wait()
+    loads[6].wait()
     loads[7].wait()
-    moe = reduce_scatter(
-        lambda x: dot(act, wd[:, columns(x)]) * share, m_buf, m_rx, m_sum, m_in, mcs, mcr, mrs_s, mrs_r
-    )
-    out = (resid.astype(F32) + moe).astype(BF)
+
+    def experts(h):
+        squares = jnp.zeros((32, 1), F32)
+        gate = jnp.zeros((32, 256), F32)
+        up = jnp.zeros((32, 256), F32)
+        for de in (0, 1, 3, 2):
+            x = lax.rem(e + 4 - de, 4)
+
+            @pl.when(c == h)
+            def _():
+                for dz in range(4):
+                    if de or dz:
+                        ag_send(de, dz).wait_recv()
+                ag_cross(x).start()
+
+            @pl.when(c != h)
+            def _():
+                ag_cross_come(x).wait_recv()
+
+            wide = ag[h, x].astype(F32)
+            for half in range(2):
+                part = wide[:, 8 * half : 8 * half + 8, :].reshape(32, HALF)
+                squares = squares + jnp.sum(part * part, axis=1, keepdims=True)
+                scaled = (part * gain[2 * x + half]).astype(BF)
+                rows = pl.ds(pl.multiple_of(x * 1792 + half * HALF, HALF), HALF)
+                gate = gate + dot(scaled, wg[rows, :])
+                up = up + dot(scaled, wu[rows, :])
+        norm = lax.rsqrt(squares * (1.0 / D) + 1e-6)
+        gate = gate * norm
+        up = up * norm
+        act = (gate / (1.0 + jnp.exp(-gate)) * up).astype(BF)
+        part = share[32 * h : 32 * h + 32]
+        shares(h, lambda x: dot(act, wd[:, columns(x)]) * part, m_buf, m_rx, mcs, mcr)
+        pass_on(h, m_buf, m_rx, m_sum, m_in, mcs, mcr, mrs_s, mrs_r)
+
+    experts(0)
+    experts(1)
+    moe = collect(m_sum, m_in, mrs_s, mrs_r)
+    out = (ag[c, e, z].astype(F32) + moe).astype(BF)
     out_ref[1] = jnp.concatenate([out[0:8], out[8:16]], axis=1)
 
     for x in k_own_sends:

time: 92.4 us -> 92.9 us (level)
  no operation moved by 1% of the time
where the time goes in v4:
time: 92.9 us; the launch traced here: 92.7 us
  Pallas kernels  90.6 us (98%)
  local copies, waits for them, and re-layouts  1.39 us (1%)
    pallas_call x1, Pallas kernels, on_device(): pl.pallas_call(kernel, out_shape=out, in_specs=[smem] + [vmem] * 5 + [any...  90.6 us

profile of v4, /device:TPU:1, one launch (start us, length us, event | category | flops | bytes accessed | tf_op | source)
XLA Modules:
  0.0 92.7 jit_solution(15612430209286358494)
XLA Ops:
  0.6 90.6 %shard_map.149 = bf16[2,8,1792]{2,1,0:T(8,128)(2,1)} custom-call(s32[2]{0:T(128)} %slen.1, bf16[8,1792]{1,0:T(8,128)(2,1)} %hid.1, bf16[8,576]{1,0:T(8,128)(2,1)} %newl.1, f32[8,1,896]{2,1,0:T(1,128)} %bitcast.21, s32[2,64]{1,0:T(2,128)} %bitcast.22, f32[2,64]{1,0:T(2,128)} %bitcast.23, bf16[256,576]{1,0:T(8,128)(2,1)} %bitcast.20, ...), custom_call_target="tpu_custom_call" | custom-call | tf_op jit(solution)/shard_map/pallas_call | solution.py:629
  91.3 1.4 %slice_bitcast_fusion = (bf16[8,1792]{1,0:T(8,128)(2,1)}, bf16[8,1792]{1,0:T(8,128)(2,1)}) fusion(bf16[2,8,1792]{2,1,0:T(8,128)(2,1)} %shard_map.149), kind=kLoop, calls=%fused_computation | loop fusion | bytes 114688 | tf_op jit(solution)/shard_map/squeeze | solution.py:654

commit v5 on v3

--- a/solution.py
+++ b/solution.py
@@ -69,6 +69,9 @@
     z_tx,
     z_rx,
     st_z,
+    d_rx,
+    d_st,
+    a_old,
     a_buf,
     a_rx,
     a_sum,
@@ -95,6 +98,10 @@
     zrs,
     zts,
     ztr,
+    dss,
+    dsr,
+    dts,
+    dtr,
     acs,
     acr,
     ars_s,
@@ -133,8 +140,8 @@
         pltpu.make_async_copy(wu_in, wu, ld.at[6]),
         pltpu.make_async_copy(wd_in, wd, ld.at[7]),
     ]
-    for x in loads[:3]:
-        x.start()
+    for i in (1, 0, 2):
+        loads[i].start()
 
     neighbours = [same_core(1, 0), same_core(3, 0), same_core(0, 1), same_core(0, 3), twin]
     bar = pltpu.get_barrier_semaphore()
@@ -142,6 +149,7 @@
         pl.semaphore_signal(bar, inc=1, device_id=x, device_id_type=MESH)
     loads[0].wait()
     q_all[r] = q_own[...].T
+    loads[1].wait()
     pl.semaphore_wait(bar, 5)
 
     def k_send(src, j, d):
@@ -149,7 +157,7 @@
         return remote(src, kt_all.at[2 * j + d], kss.at[2 * j + d], krs.at[2 * j + d], dev)
 
     def own_chunk(j, d):
-        return k_in.at[:, pl.ds(KC * (j if d == 0 else 3 - j), KC)]
+        return kt_own.at[:, pl.ds(KC * (j if d == 0 else 3 - j), KC)]
 
     def k_forward(j, d):
         dev = {"expert": right if d == 0 else left}
@@ -218,7 +226,6 @@
     nl[...] = jnp.zeros_like(nl)
     nl[0:8, :] = newl[...]
 
-    loads[1].wait()
     k_own[...] = kt_own[...].T
 
     def soft(s, g, vt):
@@ -362,6 +369,14 @@
             remote(st_z.at[q, 0], st_z.at[q, dz], zts.at[q, dz], ztr.at[q, dz], dev),
         ]
 
+    def direct_sends(i):
+        to = lax.rem(r + i, 8)
+        dev = {"resp": to}
+        return [
+            remote(hv_tx.at[3, lax.rem(to, 2), to // 2], d_rx.at[i], dss.at[i], dsr.at[i], dev),
+            remote(st_own.at[3], d_st.at[i], dts.at[i], dtr.at[i], dev),
+        ]
+
     def weight(st, top):
         return st[1:2, :] * jnp.exp2((st[0:1, :] - top) * SCALE2)
 
@@ -392,27 +407,53 @@
             y = y + z_rx[q, dz].astype(F32) * w[dz]
         return (y * (1.0 / (w[0] + w[1] + w[2] + w[3]))).astype(BF)
 
+    def plane_sum_direct():
+        for i in (1, 7, 2, 6, 3, 5, 4):
+            for x in direct_sends(i):
+                x.wait_recv()
+        top = st_own[3, 0:1, :]
+        for i in range(1, 8):
+            top = jnp.maximum(top, d_st[i, 0:1, :])
+        total = weight(st_own[3], top)
+        y = hv_tx[3, c, z].astype(F32) * total
+        for i in range(1, 8):
+            w = weight(d_st[i], top)
+            total = total + w
+            y = y + d_rx[i].astype(F32) * w
+        return (y * (1.0 / total)).astype(BF)
+
     s = last_scores(0)
     for q in range(4):
         nxt = last_scores(q + 1) if q < 3 else None
         finish(q, s)
-        for x in twin_sends(q):
-            x.start()
+        if q < 3:
+            for x in twin_sends(q):
+                x.start()
+        else:
+            for i in (4, 3, 5, 2, 6, 1, 7):
+                for x in direct_sends(i):
+                    x.start()
         if q > 0:
             chip_sum(q - 1)
         s = nxt
-    chip_sum(3)
 
     col, row = iota((GROUP, 64), 1), iota((GROUP, 64), 0)
     want = ((row % 16) // 8) * 32 + (row // 128) * 8 + row % 8
     gather = jnp.where(col == want, 1.0, 0.0).astype(BF)
     keep = (iota((128, GROUP), 0) // 16) == ((iota((128, GROUP), 1) % 128) // 16)
-    lhs = []
-    for hb in range(4):
-        piece = plane_sum(hb)
-        piece = jnp.concatenate([piece] * 8, axis=0)
-        lhs.append(dot(jnp.where(keep, piece, jnp.zeros_like(piece)), gather))
-    lhs = jnp.concatenate(lhs, axis=0).T.astype(BF)
+
+    def spread(y):
+        y = jnp.concatenate([y] * 8, axis=0)
+        return dot(jnp.where(keep, y, jnp.zeros_like(y)), gather).T.astype(BF)
+
+    def columns(x):
+        return pl.ds(pl.multiple_of(x * 1792, 128), 1792)
+
+    loads[4].wait()
+    early = jnp.concatenate([spread(plane_sum(q)) for q in range(3)], axis=1)
+    for x in range(4):
+        a_old[x] = dot(early, wo[0:384, 1792 * x : 1792 * (x + 1)])
+    late = spread(plane_sum_direct())
 
     def core_send(buf, rx, ssem, rsem, x):
         return remote(buf.at[1 - c, x], rx.at[x], ssem.at[x], rsem.at[x], twin)
@@ -447,19 +488,15 @@
             last = de
         pass_on(last)
         out = total_buf[e, z].astype(F32)
-        for de in (2, 1, 3, 0):
-            for dz in (2, 1, 3, 0):
+        for de in (0, 1, 3, 2):
+            for dz in (0, 1, 3, 2):
                 if de or dz:
                     scatter_send(total_buf, landing, ss, sr, de, dz).wait_recv()
                     out = out + landing[dz * 4 + de].astype(F32)
         return out
 
-    def columns(x):
-        return pl.ds(pl.multiple_of(x * 1792, 128), 1792)
-
-    loads[4].wait()
     attended = reduce_scatter(
-        lambda x: dot(lhs, wo[:, columns(x)]), a_buf, a_rx, a_sum, a_in, acs, acr, ars_s, ars_r
+        lambda x: a_old[x] + dot(late, wo[384:512, columns(x)]), a_buf, a_rx, a_sum, a_in, acs, acr, ars_s, ars_r
     ).astype(BF)
     hidden = jnp.concatenate([hid[:, :HALF], hid[:, HALF:]], axis=0)
     resid = (hidden.astype(F32) + attended.astype(F32)).astype(BF)
@@ -473,8 +510,8 @@
     def ag_cross(x):
         return remote(ag.at[c, x], ag.at[c, x], agc_s.at[x], agc_r.at[x], twin)
 
-    for de in (0, 1, 3, 2):
-        for dz in range(4):
+    for de in (2, 1, 3, 0):
+        for dz in (2, 1, 3, 0):
             if de or dz:
                 ag_send(de, dz).start()
 
@@ -497,7 +534,7 @@
         return squares, gate, up
 
     last = None
-    for de in (0, 1, 3, 2):
+    for de in (2, 1, 3, 0):
         for dz in range(4):
             if de or dz:
                 ag_send(de, dz).wait_recv()
@@ -533,7 +570,10 @@
         q_send(i).wait_send()
     for i in range(5):
         q_cross(i).wait_send()
-    for q in range(4):
+    for i in range(1, 8):
+        for x in direct_sends(i):
+            x.wait_send()
+    for q in range(3):
         for x in twin_sends(q):
             x.wait_send()
         for dz in range(1, 4):
@@ -599,6 +639,9 @@
         pltpu.VMEM((4, 4, 16, GROUP), BF),
         pltpu.VMEM((4, 4, 16, GROUP), BF),
         pltpu.VMEM((4, 4, 2, GROUP), F32),
+        pltpu.VMEM((8, 16, GROUP), BF),
+        pltpu.VMEM((8, 2, GROUP), F32),
+        pltpu.VMEM((4, 64, 1792), F32),
         pltpu.VMEM((2, 4, 4) + block, BF),
         pltpu.VMEM((4, 4) + block, BF),
         pltpu.VMEM((4, 4) + block, BF),
@@ -611,7 +654,7 @@
     ]
     scratch += [sem((n,)) for n in (8, 14, 14, 4, 4, 5, 5)]
     scratch += [pltpu.SemaphoreType.REGULAR, pltpu.SemaphoreType.REGULAR]
-    scratch += [sem((4,))] * 4 + [sem((4, 4))] * 4
+    scratch += [sem((4,))] * 4 + [sem((4, 4))] * 4 + [sem((8,))] * 4
     scratch += [sem((n,)) for n in (4, 4, 16, 16, 16, 16, 4, 4, 4, 4, 16, 16)]
     both = pl.pallas_call(
         kernel,

time: 92.4 us -> 94.4 us (1.022)
  Pallas kernels: 90.1 us -> 92.1 us
    pallas_call x1, Pallas kernels: 90.1 us -> 92.1 us  [on_device(): pl.pallas_call(kernel, out_shape=out, in_specs=[smem] + [vmem] * 5 + [any...]
where the time goes in v5:
time: 94.4 us; the launch traced here: 94.1 us
  Pallas kernels  92.1 us (98%)
  local copies, waits for them, and re-layouts  1.39 us (1%)
    pallas_call x1, Pallas kernels, on_device(): pl.pallas_call(kernel, out_shape=out, in_specs=[smem] + [vmem] * 5 + [any...  92.1 us

profile of v5, /device:TPU:1, one launch (start us, length us, event | category | flops | bytes accessed | tf_op | source)
XLA Modules:
  0.0 94.1 jit_solution(7026472146080791253)
XLA Ops:
  0.6 92.1 %shard_map.149 = bf16[2,8,1792]{2,1,0:T(8,128)(2,1)} custom-call(s32[2]{0:T(128)} %slen.1, bf16[8,1792]{1,0:T(8,128)(2,1)} %hid.1, bf16[8,576]{1,0:T(8,128)(2,1)} %newl.1, f32[8,1,896]{2,1,0:T(1,128)} %bitcast.21, s32[2,64]{1,0:T(2,128)} %bitcast.22, f32[2,64]{1,0:T(2,128)} %bitcast.23, bf16[256,576]{1,0:T(8,128)(2,1)} %bitcast.20, ...), custom_call_target="tpu_custom_call" | custom-call | tf_op jit(solution)/shard_map/pallas_call | solution.py:659
  92.7 1.4 %slice_bitcast_fusion = (bf16[8,1792]{1,0:T(8,128)(2,1)}, bf16[8,1792]{1,0:T(8,128)(2,1)}) fusion(bf16[2,8,1792]{2,1,0:T(8,128)(2,1)} %shard_map.149), kind=kLoop, calls=%fused_computation | loop fusion | bytes 114688 | tf_op jit(solution)/shard_map/squeeze | solution.py:684

commit v6 on v3

--- a/solution.py
+++ b/solution.py
@@ -69,6 +69,7 @@
     z_tx,
     z_rx,
     st_z,
+    a_old,
     a_buf,
     a_rx,
     a_sum,
@@ -133,13 +134,12 @@
         pltpu.make_async_copy(wu_in, wu, ld.at[6]),
         pltpu.make_async_copy(wd_in, wd, ld.at[7]),
     ]
-    for x in loads[:3]:
-        x.start()
-
     neighbours = [same_core(1, 0), same_core(3, 0), same_core(0, 1), same_core(0, 3), twin]
     bar = pltpu.get_barrier_semaphore()
     for x in neighbours:
         pl.semaphore_signal(bar, inc=1, device_id=x, device_id_type=MESH)
+    for x in loads[:3]:
+        x.start()
     loads[0].wait()
     q_all[r] = q_own[...].T
     pl.semaphore_wait(bar, 5)
@@ -407,12 +407,19 @@
     want = ((row % 16) // 8) * 32 + (row // 128) * 8 + row % 8
     gather = jnp.where(col == want, 1.0, 0.0).astype(BF)
     keep = (iota((128, GROUP), 0) // 16) == ((iota((128, GROUP), 1) % 128) // 16)
-    lhs = []
-    for hb in range(4):
-        piece = plane_sum(hb)
-        piece = jnp.concatenate([piece] * 8, axis=0)
-        lhs.append(dot(jnp.where(keep, piece, jnp.zeros_like(piece)), gather))
-    lhs = jnp.concatenate(lhs, axis=0).T.astype(BF)
+
+    def spread(y):
+        y = jnp.concatenate([y] * 8, axis=0)
+        return dot(jnp.where(keep, y, jnp.zeros_like(y)), gather).T.astype(BF)
+
+    def columns(x):
+        return pl.ds(pl.multiple_of(x * 1792, 128), 1792)
+
+    loads[4].wait()
+    early = jnp.concatenate([spread(plane_sum(q)) for q in range(3)], axis=1)
+    for x in range(4):
+        a_old[x] = dot(early, wo[0:384, 1792 * x : 1792 * (x + 1)])
+    late = spread(plane_sum(3))
 
     def core_send(buf, rx, ssem, rsem, x):
         return remote(buf.at[1 - c, x], rx.at[x], ssem.at[x], rsem.at[x], twin)
@@ -428,7 +435,7 @@
                 rows = tile[32 * cc + 8 * g : 32 * cc + 8 * g + 8, :]
                 buf[cc, x, g] = jnp.concatenate([rows[:, :HALF], rows[:, HALF:]], axis=0).astype(BF)
 
-    def reduce_scatter(tile, buf, rx, total_buf, landing, cs, cr, ss, sr):
+    def reduce_scatter(tile, buf, rx, total_buf, landing, cs, cr, ss, sr, meanwhile):
         def pass_on(de):
             x = lax.rem(e + de, 4)
             core_send(buf, rx, cs, cr, x).wait_recv()
@@ -446,20 +453,35 @@
                 pass_on(last)
             last = de
         pass_on(last)
+        meanwhile()
         out = total_buf[e, z].astype(F32)
-        for de in (2, 1, 3, 0):
-            for dz in (2, 1, 3, 0):
+        for de in (0, 1, 3, 2):
+            for dz in (0, 1, 3, 2):
                 if de or dz:
                     scatter_send(total_buf, landing, ss, sr, de, dz).wait_recv()
                     out = out + landing[dz * 4 + de].astype(F32)
         return out
 
-    def columns(x):
-        return pl.ds(pl.multiple_of(x * 1792, 128), 1792)
-
-    loads[4].wait()
+    def sent_first():
+        for x in k_own_sends:
+            x.wait_send()
+        for j in range(2):
+            for d in range(2):
+                for x in k_forward(j, d):
+                    x.wait_send()
+        for i in range(4):
+            q_send(i).wait_send()
+        for i in range(5):
+            q_cross(i).wait_send()
+        for q in range(4):
+            for x in twin_sends(q):
+                x.wait_send()
+            for dz in range(1, 4):
+                for x in z_sends(q, dz):
+                    x.wait_send()
+
     attended = reduce_scatter(
-        lambda x: dot(lhs, wo[:, columns(x)]), a_buf, a_rx, a_sum, a_in, acs, acr, ars_s, ars_r
+        lambda x: a_old[x] + dot(late, wo[384:512, columns(x)]), a_buf, a_rx, a_sum, a_in, acs, acr, ars_s, ars_r, sent_first
     ).astype(BF)
     hidden = jnp.concatenate([hid[:, :HALF], hid[:, HALF:]], axis=0)
     resid = (hidden.astype(F32) + attended.astype(F32)).astype(BF)
@@ -474,7 +496,7 @@
         return remote(ag.at[c, x], ag.at[c, x], agc_s.at[x], agc_r.at[x], twin)
 
     for de in (0, 1, 3, 2):
-        for dz in range(4):
+        for dz in (2, 1, 3, 0):
             if de or dz:
                 ag_send(de, dz).start()
 
@@ -517,36 +539,22 @@
     here = tok == ((row // 8) % 4) * 16 + (row // 32) * 8 + row % 8
     share = jnp.sum(jnp.where(here, share, 0.0), axis=1, keepdims=True)
     loads[7].wait()
+    def sent_last():
+        for x in range(4):
+            core_send(a_buf, a_rx, acs, acr, x).wait_send()
+            ag_cross(x).wait_send()
+            core_send(m_buf, m_rx, mcs, mcr, x).wait_send()
+        for i in range(1, 16):
+            scatter_send(a_sum, a_in, ars_s, ars_r, i % 4, i // 4).wait_send()
+            ag_send(i % 4, i // 4).wait_send()
+        for i in (10, 6, 14, 9, 11, 5, 7, 13, 15, 2, 8, 1, 3, 4, 12):
+            scatter_send(m_sum, m_in, mrs_s, mrs_r, i % 4, i // 4).wait_send()
+
     moe = reduce_scatter(
-        lambda x: dot(act, wd[:, columns(x)]) * share, m_buf, m_rx, m_sum, m_in, mcs, mcr, mrs_s, mrs_r
+        lambda x: dot(act, wd[:, columns(x)]) * share, m_buf, m_rx, m_sum, m_in, mcs, mcr, mrs_s, mrs_r, sent_last
     )
     out = (resid.astype(F32) + moe).astype(BF)
     out_ref[1] = jnp.concatenate([out[0:8], out[8:16]], axis=1)
-
-    for x in k_own_sends:
-        x.wait_send()
-    for j in range(2):
-        for d in range(2):
-            for x in k_forward(j, d):
-                x.wait_send()
-    for i in range(4):
-        q_send(i).wait_send()
-    for i in range(5):
-        q_cross(i).wait_send()
-    for q in range(4):
-        for x in twin_sends(q):
-            x.wait_send()
-        for dz in range(1, 4):
-            for x in z_sends(q, dz):
-                x.wait_send()
-    for x in range(4):
-        core_send(a_buf, a_rx, acs, acr, x).wait_send()
-        core_send(m_buf, m_rx, mcs, mcr, x).wait_send()
-        ag_cross(x).wait_send()
-    for i in range(1, 16):
-        scatter_send(a_sum, a_in, ars_s, ars_r, i % 4, i // 4).wait_send()
-        scatter_send(m_sum, m_in, mrs_s, mrs_r, i % 4, i // 4).wait_send()
-        ag_send(i % 4, i // 4).wait_send()
 
 
 def on_device(
@@ -599,6 +607,7 @@
         pltpu.VMEM((4, 4, 16, GROUP), BF),
         pltpu.VMEM((4, 4, 16, GROUP), BF),
         pltpu.VMEM((4, 4, 2, GROUP), F32),
+        pltpu.VMEM((4, 64, 1792), F32),
         pltpu.VMEM((2, 4, 4) + block, BF),
         pltpu.VMEM((4, 4) + block, BF),
         pltpu.VMEM((4, 4) + block, BF),

time: 92.4 us -> 91.7 us (level)
  no operation moved by 1% of the time
where the time goes in v6:
time: 91.7 us; the launch traced here: 91.5 us
  Pallas kernels  89.5 us (98%)
  local copies, waits for them, and re-layouts  1.39 us (2%)
    pallas_call x1, Pallas kernels, on_device(): pl.pallas_call(kernel, out_shape=out, in_specs=[smem] + [vmem] * 5 + [any...  89.5 us

profile of v6, /device:TPU:1, one launch (start us, length us, event | category | flops | bytes accessed | tf_op | source)
XLA Modules:
  0.0 91.5 jit_solution(7086191606455567216)
XLA Ops:
  0.6 89.5 %shard_map.149 = bf16[2,8,1792]{2,1,0:T(8,128)(2,1)} custom-call(s32[2]{0:T(128)} %slen.1, bf16[8,1792]{1,0:T(8,128)(2,1)} %hid.1, bf16[8,576]{1,0:T(8,128)(2,1)} %newl.1, f32[8,1,896]{2,1,0:T(1,128)} %bitcast.21, s32[2,64]{1,0:T(2,128)} %bitcast.22, f32[2,64]{1,0:T(2,128)} %bitcast.23, bf16[256,576]{1,0:T(8,128)(2,1)} %bitcast.20, ...), custom_call_target="tpu_custom_call" | custom-call | tf_op jit(solution)/shard_map/pallas_call | solution.py:625
  90.1 1.4 %slice_bitcast_fusion = (bf16[8,1792]{1,0:T(8,128)(2,1)}, bf16[8,1792]{1,0:T(8,128)(2,1)}) fusion(bf16[2,8,1792]{2,1,0:T(8,128)(2,1)} %shard_map.149), kind=kLoop, calls=%fused_computation | loop fusion | bytes 114688 | tf_op jit(solution)/shard_map/squeeze | solution.py:650

commit v7 on v6

--- a/solution.py
+++ b/solution.py
@@ -486,7 +486,6 @@
     hidden = jnp.concatenate([hid[:, :HALF], hid[:, HALF:]], axis=0)
     resid = (hidden.astype(F32) + attended.astype(F32)).astype(BF)
     ag[c, e, z] = resid
-    out_ref[0] = jnp.concatenate([attended[0:8], attended[8:16]], axis=1)
 
     def ag_send(de, dz):
         i = dz * 4 + de
@@ -500,8 +499,15 @@
             if de or dz:
                 ag_send(de, dz).start()
 
+    out_ref[0] = jnp.concatenate([attended[0:8], attended[8:16]], axis=1)
+    picked = jnp.where(gids[...] == e, gwts[...], 0.0)
+    share = 2.5 * jnp.sum(picked, axis=0, keepdims=True) / jnp.sum(gwts[...], axis=0, keepdims=True)
+    row, tok = iota((64, 64), 0), iota((64, 64), 1)
+    here = tok == ((row // 8) % 4) * 16 + (row // 32) * 8 + row % 8
+    share = jnp.sum(jnp.where(here, share, 0.0), axis=1, keepdims=True)
     loads[5].wait()
     loads[6].wait()
+    loads[7].wait()
     squares = jnp.zeros((64, 1), F32)
     gate = jnp.zeros((64, 256), F32)
     up = jnp.zeros((64, 256), F32)
@@ -533,12 +539,6 @@
     up = up * norm
     act = (gate / (1.0 + jnp.exp(-gate)) * up).astype(BF)
 
-    picked = jnp.where(gids[...] == e, gwts[...], 0.0)
-    share = 2.5 * jnp.sum(picked, axis=0, keepdims=True) / jnp.sum(gwts[...], axis=0, keepdims=True)
-    row, tok = iota((64, 64), 0), iota((64, 64), 1)
-    here = tok == ((row // 8) % 4) * 16 + (row // 32) * 8 + row % 8
-    share = jnp.sum(jnp.where(here, share, 0.0), axis=1, keepdims=True)
-    loads[7].wait()
     def sent_last():
         for x in range(4):
             core_send(a_buf, a_rx, acs, acr, x).wait_send()

time: 91.7 us -> 91.7 us (level)
  no operation moved by 1% of the time
where the time goes in v7:
time: 91.7 us; the launch traced here: 91.4 us
  Pallas kernels  89.4 us (97%)
  local copies, waits for them, and re-layouts  1.39 us (2%)
    pallas_call x1, Pallas kernels, on_device(): pl.pallas_call(kernel, out_shape=out, in_specs=[smem] + [vmem] * 5 + [any...  89.4 us

profile of v7, /device:TPU:1, one launch (start us, length us, event | category | flops | bytes accessed | tf_op | source)
XLA Modules:
  0.0 91.4 jit_solution(9764469092083543056)
XLA Ops:
  0.6 89.4 %shard_map.149 = bf16[2,8,1792]{2,1,0:T(8,128)(2,1)} custom-call(s32[2]{0:T(128)} %slen.1, bf16[8,1792]{1,0:T(8,128)(2,1)} %hid.1, bf16[8,576]{1,0:T(8,128)(2,1)} %newl.1, f32[8,1,896]{2,1,0:T(1,128)} %bitcast.21, s32[2,64]{1,0:T(2,128)} %bitcast.22, f32[2,64]{1,0:T(2,128)} %bitcast.23, bf16[256,576]{1,0:T(8,128)(2,1)} %bitcast.20, ...), custom_call_target="tpu_custom_call" | custom-call | tf_op jit(solution)/shard_map/pallas_call | solution.py:625
  90.0 1.4 %slice_bitcast_fusion = (bf16[8,1792]{1,0:T(8,128)(2,1)}, bf16[8,1792]{1,0:T(8,128)(2,1)}) fusion(bf16[2,8,1792]{2,1,0:T(8,128)(2,1)} %shard_map.149), kind=kLoop, calls=%fused_computation | loop fusion | bytes 114688 | tf_op jit(solution)/shard_map/squeeze | solution.py:650
